TPU v7x, 512 devices: a whole 4x4x16 slice. The times are simulated.
512 devices in a mesh: ctx: 64 (over y, z), tp: 8 (over x, core).
Axes of the slice: x: 4, y: 4, z: 16, core: 2. Of those that a mesh axis runs over, the one named last changes fastest.
Arguments:
- grad_out: bfloat16 [8192, 4096], P('ctx', 'tp'), may hold values from -6 to 6
- gate: bfloat16 [8192, 4096], P('ctx', 'tp'), may hold values from -6 to 6
- conv_input: bfloat16 [8192, 4096], P('ctx', 'tp'), may hold values from -6 to 6
- out_weight: bfloat16 [4096, 4096], P('tp', 'ctx'), may hold values from -0.09375 to 0.09375
- residues: float32 [16, 4096], P(None, 'tp'), may hold values from -0.12 to 0.12
- rates: float32 [16, 4096], P(None, 'tp'), may hold values from 6.1035156e-05 to 0.04
Outputs:
- input_grad: bfloat16 [8192, 4096], P('ctx', 'tp')
- residue_grad: float32 [16, 4096], P(None, 'tp')
All inputs are finite; a program needn't handle non-finite values.
Results may differ from a plain program's by a relative error of at most 0.0027.
Values may be sent and summed in bfloat16 or wider, within the bound.
A program may use at most 64 MiB of HBM per device.

v0:
```python
import jax
import jax.numpy as jnp
from jax import lax
from jax.sharding import PartitionSpec as P


def carried_in(part, axis, combine, identity, reverse):
    count = lax.axis_size(axis)
    place = lax.axis_index(axis)
    ahead = count - 1 - place if reverse else place
    gathered = jax.tree.map(lambda a: lax.all_gather(a, axis), part)
    state = jax.tree.map(lambda a, e: jnp.zeros_like(a) + jnp.asarray(e, a.dtype), part, identity)

    def one(lap, state):
        source = count - 1 - lap if reverse else lap
        return combine(
            state, jax.tree.map(lambda a: lax.dynamic_index_in_dim(a, source, 0, False), gathered)
        )

    return lax.fori_loop(0, ahead, one, state)


def chain_join(earlier, later):
    return (earlier[0] * later[0], earlier[1] * later[0] + later[1])


def local(grad_out, gate, conv_input, out_weight, residues, rates):
    rows = grad_out.shape[0]
    width = grad_out.shape[1]
    modes = residues.shape[0]
    whole = lax.all_gather(grad_out, "tp", axis=1, tiled=True)
    grad_y = lax.dot_general(
        whole,
        lax.all_gather(out_weight, "ctx", axis=1, tiled=True),
        (((1,), (1,)), ((), ())),
        preferred_element_type=jnp.float32,
    )
    grad_conv = gate.astype(jnp.float32) * grad_y
    values = conv_input.astype(jnp.float32)
    steps = jnp.arange(rows, dtype=jnp.float32)
    upper = (steps[:, None] <= steps[None, :]).astype(jnp.float32)
    lower = upper.T
    grouped_rates = rates.reshape(modes // 4, 4, width)
    grouped_res = residues.reshape(modes // 4, 4, width)

    def local_group(acc, pair):
        rate_group, res_group = pair
        falling = jnp.exp(-rate_group[None] * steps[:, None, None])
        rising = jnp.exp(rate_group[None] * steps[:, None, None])
        weighted = (grad_conv[:, None, :] * falling).reshape(rows, 4 * width)
        tails = (
            jnp.dot(upper, weighted, precision=lax.Precision.HIGHEST).reshape(rows, 4, width)
            * rising
        )
        acc = acc + jnp.einsum("kmc,mc->kc", tails, res_group)
        lifted = (values[:, None, :] * rising).reshape(rows, 4 * width)
        heads = (
            jnp.dot(lower, lifted, precision=lax.Precision.HIGHEST).reshape(rows, 4, width)
            * falling
        )
        ending = heads[rows - 1]
        inner = jnp.sum(grad_conv[:, None, :] * heads, axis=0)
        return (acc, (tails[0], ending, inner))

    near, (starts, endings, inners) = lax.scan(
        local_group, jnp.zeros((rows, width), jnp.float32), (grouped_rates, grouped_res)
    )
    starts = starts.reshape(modes, width)
    endings = endings.reshape(modes, width)
    inners = inners.reshape(modes, width)
    block_decay = jnp.exp(-rates * jnp.float32(rows))
    identity = (jnp.ones((modes, width), jnp.float32), jnp.zeros((modes, width), jnp.float32))
    _, incoming = carried_in((block_decay, starts), "ctx", chain_join, identity, True)
    step_decay = jnp.exp(-rates)
    _, before = carried_in((block_decay, endings), "ctx", chain_join, identity, False)
    cross_term = before * step_decay * starts
    summed = lax.psum(inners + cross_term, "ctx")
    residue_grad = summed / jnp.float32(rows * lax.axis_size("ctx"))
    weighted_in = (residues * incoming).reshape(modes // 4, 4, width)

    def far_group(acc, pair):
        rate_group, scaled = pair
        factor = jnp.exp(-rate_group[None] * (jnp.float32(rows) - steps)[:, None, None])
        return (acc + jnp.einsum("kmc,mc->kc", factor, scaled), None)

    far, _ = lax.scan(
        far_group, jnp.zeros((rows, width), jnp.float32), (grouped_rates, weighted_in)
    )
    input_grad = (near + far).astype(jnp.bfloat16)
    return (input_grad, residue_grad)


def solution(mesh):
    placed = (
        P("ctx", "tp"),
        P("ctx", "tp"),
        P("ctx", "tp"),
        P("tp", "ctx"),
        P(None, "tp"),
        P(None, "tp"),
    )
    return jax.shard_map(
        local,
        mesh=mesh,
        in_specs=placed,
        out_specs=(P("ctx", "tp"), P(None, "tp")),
        check_vma=False,
    )
```

profile of v0, /device:TPU:4, one launch (start us, length us, event | category | flops | bytes accessed | tf_op | source)
XLA Modules:
  0.0 866.2 jit_solution(7574068026459360362)
XLA Ops:
  8.7 1.4 multiply_exponential_fusion
  11.0 1.0 copy.18
  12.8 31.8 %all-gather.7.cloned.1.call-done = bf16[128,4096]{1,0:T(8,128)(2,1)} async-done(((bf16[128,512]{1,0:T(8,128)(2,1)}), bf16[128,4096]{1,0:T(8,128)(2,1)}) %all-gather.7.cloned.1.call-update) | async-done | bytes 1048592 | tf_op jit(solution)/shard_map/all_gather | solution.py:31
  44.6 150.6 %all-gather.9.cloned.1.call-done = bf16[512,4096]{0,1:T(8,128)(2,1)} async-done(((bf16[512,64]{0,1:T(8,128)(2,1)}), bf16[512,4096]{0,1:T(8,128)(2,1)}) %all-gather.9.cloned.1.call-update) | async-done | bytes 4194320 | tf_op jit(solution)/shard_map/all_gather | solution.py:34
  195.1 3.2 convolution_multiply_fusion
  198.5 23.3 %while.58 = (s32[]{:T(128)}, f32[128,512]{1,0:T(8,128)S(1)}, f32[4,4,512]{2,1,0:T(4,128)S(1)}, f32[4,4,512]{2,1,0:T(4,128)}, f32[4,4,512]{2,1,0:T(4,128)}, /*ind...) while((s32[]{:T(128)}, f32[128,512]{1,0:T(8,128)S(1)}, ...), condition=%wide.region_2.3_spmd.clone.clone, body=%wide.region_0.2_spmd.clone.clone.sunk | while | flops 808329216 | bytes 10740863 | solution.py:65
  198.6 1.2 fusion.32
  199.8 1.0 fusion.33
  204.4 1.2 fusion.32
  205.7 1.0 fusion.33
  210.3 1.2 fusion.32
  211.5 1.0 fusion.33
  216.1 1.2 fusion.32
  217.3 1.0 fusion.33
  221.8 1.4 all_gather_reshape.7
  224.7 109.0 %all-gather.15.cloned.1.call-done = f32[1024,512]{1,0:T(8,128)} async-done(((f32[16,512]{1,0:T(8,128)}), f32[1024,512]{1,0:T(8,128)}) %all-gather.15.cloned.1.call-update) | async-done | bytes 2097168 | tf_op jit(solution)/shard_map/all_gather | solution.py:11
  333.7 139.8 %all-gather.13.cloned.1.call-done = f32[64,16,512]{2,1,0:T(8,128)} async-done(((f32[1,16,512]{2,1,0:T(8,128)}), f32[64,16,512]{2,1,0:T(8,128)}) %all-gather.13.cloned.1.call-update) | async-done | bytes 2097168 | tf_op jit(solution)/shard_map/all_gather | solution.py:11
  473.6 329.1 %psum.7 = f32[16,512]{1,0:T(8,128)S(1)} all-reduce(f32[16,512]{1,0:T(8,128)S(1)} %multiply_add_fusion), channel_id=1, replica_groups=mesh['ctx'=64,'tp'=8] {'ctx'}, use_global_device_ids=true, to_apply=%region_9.10 | all-reduce | flops 8192 | bytes 65536 | tf_op jit(solution)/shard_map/psum | solution.py:77
  803.3 51.4 %while.55 = (s32[]{:T(128)}, f32[16,512]{1,0:T(8,128)S(1)}, s32[]{:T(128)}, f32[64,16,512]{2,1,0:T(8,128)}, f32[64,16,512]{2,1,0:T(8,128)}, /*index=5*/s32[]{:T(128)}, s32[]{:T(128)}, s32[]{:T(128)}, s32[]{:T(128)}) while((s32[]{:T(128)}, f32[16,512]{1,0:T(8,128)S(1)}, s32[]{:T(128)}, f32[64,16,512]{2,1,0:T(8,128)}, f32[64,16,512]{2,1,0:T(8,128)}, ...), condition=%wide.region_4.5_spmd, body=%wide.region_3.4_spmd.sunk | while | flops 16390 | bytes 131215 | solution.py:20
  804.1 0.8 bitcast_add_fusion.8
  804.9 0.8 bitcast_add_fusion.8
  805.7 0.8 bitcast_add_fusion.8
  806.6 0.8 bitcast_add_fusion.8
  807.4 0.8 bitcast_add_fusion.8
  808.2 0.8 bitcast_add_fusion.8
  809.0 0.8 bitcast_add_fusion.8
  809.8 0.8 bitcast_add_fusion.8
  810.7 0.8 bitcast_add_fusion.8
  811.5 0.8 bitcast_add_fusion.8
  812.3 0.8 bitcast_add_fusion.8
  813.1 0.8 bitcast_add_fusion.8
  813.9 0.8 bitcast_add_fusion.8
  814.7 0.8 bitcast_add_fusion.8
  815.6 0.8 bitcast_add_fusion.8
  816.4 0.8 bitcast_add_fusion.8
  817.2 0.8 bitcast_add_fusion.8
  818.0 0.8 bitcast_add_fusion.8
  818.8 0.8 bitcast_add_fusion.8
  819.6 0.8 bitcast_add_fusion.8
  820.5 0.8 bitcast_add_fusion.8
  821.3 0.8 bitcast_add_fusion.8
  822.1 0.8 bitcast_add_fusion.8
  822.9 0.8 bitcast_add_fusion.8
  823.7 0.8 bitcast_add_fusion.8
  824.5 0.8 bitcast_add_fusion.8
  825.4 0.8 bitcast_add_fusion.8
  826.2 0.8 bitcast_add_fusion.8
  827.0 0.8 bitcast_add_fusion.8
  827.8 0.8 bitcast_add_fusion.8
  828.6 0.8 bitcast_add_fusion.8
  831.9 0.8 bitcast_add_fusion.8
  832.7 0.8 bitcast_add_fusion.8
  833.5 0.8 bitcast_add_fusion.8
  840.1 0.8 bitcast_add_fusion.8
  840.9 0.8 bitcast_add_fusion.8
  841.7 0.8 bitcast_add_fusion.8
  847.4 0.8 bitcast_add_fusion.8
  848.2 0.8 bitcast_add_fusion.8
  849.0 0.8 bitcast_add_fusion.8
  854.8 4.1 while.57
  854.8 0.9 multiply_reduce_fusion.4
  855.9 0.9 multiply_reduce_fusion.4
  856.9 0.9 multiply_reduce_fusion.4
  857.9 0.9 multiply_reduce_fusion.4
  (126 shorter events, 38.9 us)
Async XLA Ops:
  7.2 37.4 %all-gather.7.cloned.1.call-start = ((), (), s32[]{:S(2)}) async-start(), calls=%async_computation | async-start | bytes 1179648 | tf_op jit(solution)/shard_map/all_gather | solution.py:31
  7.9 187.2 %all-gather.9.cloned.1.call-start = ((), (), s32[]{:S(2)}) async-start(), calls=%async_computation.1 | async-start | bytes 4259840 | tf_op jit(solution)/shard_map/all_gather | solution.py:34
  8.6 325.1 %all-gather.15.cloned.1.call-start = ((), (), s32[]{:S(2)}) async-start(), calls=%async_computation.4 | async-start | bytes 2129920 | tf_op jit(solution)/shard_map/all_gather | solution.py:11
  10.1 463.4 %all-gather.13.cloned.1.call-start = ((), (), s32[]{:S(2)}) async-start(), calls=%async_computation.3 | async-start | bytes 2129920 | tf_op jit(solution)/shard_map/all_gather | solution.py:11
  198.5 275.1 %copy-start = (f32[16,512]{1,0:T(8,128)S(1)}, f32[16,512]{1,0:T(8,128)}, u32[]{:S(2)}) copy-start(f32[16,512]{1,0:T(8,128)} %param.19) | copy-start | bytes 98308
  221.8 633.0 %copy-start.1 = (f32[16,512]{1,0:T(8,128)S(1)}, f32[16,512]{1,0:T(8,128)}, u32[]{:S(2)}) copy-start(f32[16,512]{1,0:T(8,128)} %param.18) | copy-start | bytes 98308
  223.2 580.1 %all-gather.11.cloned.1.call-start = ((), (), s32[]{:S(2)}) async-start(), calls=%async_computation.2 | async-start | bytes 2129920 | tf_op jit(solution)/shard_map/all_gather | solution.py:11
Sparse Core Ops, SparseCore 0:
  10.1 34.3 all-gather.6
  47.5 147.5 all-gather.8
  198.1 135.5 all-gather.14
  336.5 136.9 all-gather.12
  476.3 136.9 all-gather.10
where the time goes:
time: 871 us; the launch traced here: 866 us
  waiting for transfers between devices  433 us (50%)
  blocking collectives  329 us (38%)
  other arithmetic  62.3 us (7%)
  local copies, waits for them, and re-layouts  13.9 us (2%)
  between operations  13.9 us (2%)
  matrix products  12 us (1%)
    psum x1, blocking collectives, local(): summed = lax.psum(inners + cross_term, 'ctx')  329 us
    all_gather x3, waiting for transfers between devices, carried_in(): gathered = jax.tree.map(lambda a: lax.all_gather(a, axis), part)  249 us
    all_gather x1, waiting for transfers between devices, local(): lax.all_gather(out_weight, 'ctx', axis=1, tiled=True)  151 us
    add x63, other arithmetic, chain_join(): return (earlier[0] * later[0], earlier[1] * later[0] + later[1])  49.8 us
    all_gather x1, waiting for transfers between devices, local(): whole = lax.all_gather(grad_out, 'tp', axis=1, tiled=True)  31.8 us
  transfers between devices with their start and end apart: 5, of which 4 were waited for; matrix products, arithmetic and copies ran while one was open for 4% of the time, Pallas kernels for 0%

commit v1 on v0

v1 whole, which is shorter than its diff:
```python
import jax
import jax.numpy as jnp
from jax import lax
from jax.experimental import pallas as pl
from jax.experimental.pallas import tpu as pltpu
from jax.sharding import PartitionSpec as P

MESH = pl.DeviceIdType.MESH
F32 = jnp.float32
BF16 = jnp.bfloat16
MODES = 16
NX = 4
NY = 4
NZ = 16
ROWS = 128
WIDE = 512
LANES = 128
SEG = 64
LENGTH = 8192


def kernel(
    go, gate, conv, weight, residues, rates,
    out, rout,
    gobuf, wbuf, wt, gt, cv, rt, rs,
    dec, resb, gc, cvf, near, starts, arrived, ends, ends_in, backs, incoming, rowsum, rowsum_in,
    outf, outb, rcomp,
    loc_sem, wy_s, wy_r, go_s, go_r, sib_s, sib_r, gc_s, gc_r, z_s, z_r,
    a_s, a_r, e_s, e_r, b_s, b_r, t_s, t_r, o_s, o_r, ro_s, ro_r,
):
    ctx = lax.axis_index("ctx")
    tp = lax.axis_index("tp")
    x, k = tp // 2, tp % 2
    y, z = ctx // NZ, ctx % NZ
    xp, xm, x2 = (x + 1) % NX, (x + 3) % NX, (x + 2) % NX
    yp, ym, y2 = (y + 1) % NY, (y + 3) % NY, (y + 2) % NY
    zp, zm = (z + 1) % NZ, (z + NZ - 1) % NZ

    def dev(dx=None, dy=None, dz=None, dk=None):
        xx = x if dx is None else dx
        yy = y if dy is None else dy
        zz = z if dz is None else dz
        kk = k if dk is None else dk
        return (yy * NZ + zz, xx * 2 + kk)

    near_devices = [dev(dx=xp), dev(dx=xm), dev(dy=yp), dev(dy=ym), dev(dy=y2), dev(dz=zp), dev(dz=zm), dev(dk=1 - k)]
    barrier = pltpu.get_barrier_semaphore()
    for d in near_devices:
        pl.semaphore_signal(barrier, inc=1, device_id=d, device_id_type=MESH)

    unsent = []

    def send(src, dst, ss, rs_, target):
        c = pltpu.make_async_remote_copy(
            src_ref=src, dst_ref=dst, send_sem=ss, recv_sem=rs_, device_id=target, device_id_type=MESH
        )
        c.start()
        unsent.append(c)

    def wait_in(ref, sem):
        pltpu.make_async_copy(ref, ref, sem).wait()

    cols = pl.ds(pl.multiple_of(y * LANES, LANES), LANES)
    me = x * 2 + k
    locals_ = [
        pltpu.make_async_copy(go, gobuf.at[me, y], loc_sem.at[0]),
        pltpu.make_async_copy(gate.at[:, cols], gt.at[y], loc_sem.at[1]),
        pltpu.make_async_copy(conv.at[:, cols], cv.at[y], loc_sem.at[2]),
        pltpu.make_async_copy(rates.at[:, cols], rt, loc_sem.at[3]),
        pltpu.make_async_copy(residues.at[:, cols], rs, loc_sem.at[4]),
    ]
    for c in locals_:
        c.start()
    for q in range(NY):
        wt[q] = weight[q * LANES : (q + 1) * LANES, :].astype(F32).T.astype(BF16)
    wbuf[0, z] = wt[y]
    for c in locals_:
        c.wait()
    for m in range(MODES):
        dec[m] = jnp.broadcast_to(jnp.exp(-rt[m : m + 1, :]), (8, LANES))
        resb[m] = jnp.broadcast_to(rs[m : m + 1, :], (8, LANES))

    pl.semaphore_wait(barrier, len(near_devices))

    for r in range(1, NY):
        to = (y + NY - r) % NY
        send(wt.at[to], wbuf.at[r, z], wy_s.at[r], wy_r.at[r], dev(dy=to))

    A, B = (0, 64), (64, 64)
    A0, A1, B0, B1 = (0, 32), (32, 32), (64, 32), (96, 32)
    go_slots = {}

    def go_ref(ox, oy, piece):
        return gobuf.at[ox * 2 + k, oy, pl.ds(piece[0], piece[1]), :]

    def go_send(key, ox, oy, piece, target, src=None):
        slot = go_slots.setdefault(key, len(go_slots))
        ref = go_ref(ox, oy, piece)
        send(ref if src is None else src, ref, go_s.at[slot], go_r.at[slot], target)

    def go_wait(key, ox, oy, piece):
        wait_in(go_ref(ox, oy, piece), go_r.at[go_slots[key]])

    def own(piece):
        return go.at[pl.ds(piece[0], piece[1]), :]

    go_send(("+x", "L", "A"), x, y, A, dev(dx=xp), own(A))
    go_send(("-x", "R", "A"), x, y, A, dev(dx=xm), own(A))
    go_send(("+y", "D", "B"), x, y, B, dev(dy=yp), own(B))
    go_send(("-y", "U", "B"), x, y, B, dev(dy=ym), own(B))
    go_send(("+x", "L", "B"), x, y, B, dev(dx=xp), own(B))
    go_send(("-x", "R", "B"), x, y, B, dev(dx=xm), own(B))
    go_send(("+y", "D", "A"), x, y, A, dev(dy=yp), own(A))
    go_send(("-y", "U", "A"), x, y, A, dev(dy=ym), own(A))

    sib_slots = []

    def sibling(ox, oy, src=None):
        slot = len(sib_slots)
        ref = gobuf.at[ox * 2 + k, oy]
        send(ref if src is None else src, ref, sib_s.at[slot], sib_r.at[slot], dev(dk=1 - k))
        sib_slots.append((ox, oy))

    sibling(x, y, go)

    HALVES = (0, 2)

    def z_send(way, sub, step, owner, target):
        ref = wbuf.at[pl.ds(sub, 2), owner]
        i = (way * 2 + sub // 2) * 8 + step - 1
        send(ref, ref, z_s.at[i], z_r.at[i], target)

    def z_wait(way, sub, step, owner):
        i = (way * 2 + sub // 2) * 8 + step - 1
        wait_in(wbuf.at[pl.ds(sub, 2), owner], z_r.at[i])

    def z_start(sub):
        for r in (sub, sub + 1):
            if r:
                wait_in(wbuf.at[r, z], wy_r.at[r])
        z_send(0, sub, 1, z, dev(dz=zp))
        z_send(1, sub, 1, z, dev(dz=zm))

    def z_round(step):
        for sub in HALVES:
            for way in (0, 1):
                if step == 8 and way != sub // 2:
                    continue
                owner = (z + NZ - step) % NZ if way == 0 else (z + step) % NZ
                z_wait(way, sub, step, owner)
                if step < 7 or (step == 7 and way == sub // 2):
                    z_send(way, sub, step + 1, owner, dev(dz=zp) if way == 0 else dev(dz=zm))

    z_start(0)
    z_start(2)

    for r in range(1, NY):
        to = (y + r) % NY
        tc = pl.ds(pl.multiple_of(to * LANES, LANES), LANES)
        send(gate.at[:, tc], gt.at[y], gc_s.at[r], gc_r.at[r], dev(dy=to))
        send(conv.at[:, tc], cv.at[y], gc_s.at[4 + r], gc_r.at[4 + r], dev(dy=to))

    z_round(1)
    go_wait(("+x", "L", "A"), xm, y, A)
    go_send(("+x", "X2", "A"), xm, y, A, dev(dx=xp))
    go_send(("+y", "L,D", "A"), xm, y, A, dev(dy=yp))
    go_send(("-y", "L,U", "A"), xm, y, A, dev(dy=ym))
    go_wait(("-y", "U", "B"), x, yp, B)
    go_send(("-y", "Y2", "B"), x, yp, B, dev(dy=ym))
    go_send(("+x", "U,L", "B"), x, yp, B, dev(dx=xp))
    go_send(("-x", "U,R", "B"), x, yp, B, dev(dx=xm))
    go_wait(("-x", "R", "A"), xp, y, A)
    go_send(("+y", "R,D", "A"), xp, y, A, dev(dy=yp))
    go_send(("-y", "R,U", "A"), xp, y, A, dev(dy=ym))
    go_wait(("+y", "D", "B"), x, ym, B)
    go_send(("+x", "D,L", "B"), x, ym, B, dev(dx=xp))
    go_send(("-x", "D,R", "B"), x, ym, B, dev(dx=xm))
    z_round(2)
    go_wait(("-x", "R", "B"), xp, y, B)
    go_send(("-x", "X2", "B"), xp, y, B, dev(dx=xm))
    go_wait(("+y", "D", "A"), x, ym, A)
    go_send(("+y", "Y2", "A"), x, ym, A, dev(dy=yp))
    go_wait(("+x", "L", "B"), xm, y, B)
    go_wait(("-y", "U", "A"), x, yp, A)
    sibling(xm, y)
    sibling(xp, y)
    sibling(x, ym)
    sibling(x, yp)
    z_round(3)
    go_wait(("+x", "X2", "A"), x2, y, A)
    go_send(("+y", "X2,D", "A"), x2, y, A, dev(dy=yp))
    go_send(("-y", "X2,U", "A"), x2, y, A, dev(dy=ym))
    go_wait(("-y", "Y2", "B"), x, y2, B)
    go_send(("+x", "Y2,L", "B"), x, y2, B, dev(dx=xp))
    go_send(("-x", "Y2,R", "B"), x, y2, B, dev(dx=xm))
    z_round(4)
    for col, ox in (("L", xm), ("R", xp)):
        go_wait(("+y", col + ",D", "A"), ox, ym, A)
        go_send(("+y", col + ",Y2", "A0"), ox, ym, A0, dev(dy=yp))
        go_wait(("-y", col + ",U", "A"), ox, yp, A)
        go_send(("-y", col + ",Y2", "A1"), ox, yp, A1, dev(dy=ym))
    for row, oy in (("D", ym), ("U", yp)):
        go_wait(("+x", row + ",L", "B"), xm, oy, B)
        go_send(("+x", row + ",X2", "B0"), xm, oy, B0, dev(dx=xp))
        go_wait(("-x", row + ",R", "B"), xp, oy, B)
        go_send(("-x", row + ",X2", "B1"), xp, oy, B1, dev(dx=xm))
    for ox in (xm, xp):
        for oy in (ym, yp):
            sibling(ox, oy)
    z_round(5)
    go_wait(("-x", "X2", "B"), x2, y, B)
    go_wait(("+y", "Y2", "A"), x, y2, A)
    sibling(x2, y)
    sibling(x, y2)
    z_round(6)
    for r in range(1, NY):
        src = (y + NY - r) % NY
        wait_in(gt.at[src], gc_r.at[r])
        wait_in(cv.at[src], gc_r.at[4 + r])
    for q in range(NY):
        cvf[q * ROWS : (q + 1) * ROWS, :] = cv[q].astype(F32)

    def end_step(t, sums):
        c = cvf[pl.ds(t, 8, stride=SEG), :]
        return tuple(dec[m] * (s + c) for m, s in enumerate(sums))

    zeros = tuple(jnp.zeros((8, LANES), F32) for _ in range(MODES))
    for m, s in enumerate(lax.fori_loop(0, SEG, end_step, zeros)):
        ends[m, 0] = s
    go_wait(("+y", "X2,D", "A"), x2, ym, A)
    go_send(("+y", "X2,Y2", "A0"), x2, ym, A0, dev(dy=yp))
    go_wait(("-y", "X2,U", "A"), x2, yp, A)
    go_send(("-y", "X2,Y2", "A1"), x2, yp, A1, dev(dy=ym))
    go_wait(("+x", "Y2,L", "B"), xm, y2, B)
    go_send(("+x", "Y2,X2", "B0"), xm, y2, B0, dev(dx=xp))
    go_wait(("-x", "Y2,R", "B"), xp, y2, B)
    go_send(("-x", "Y2,X2", "B1"), xp, y2, B1, dev(dx=xm))
    z_round(7)
    for col, ox in (("L", xm), ("R", xp)):
        go_wait(("+y", col + ",Y2", "A0"), ox, y2, A0)
        go_wait(("-y", col + ",Y2", "A1"), ox, y2, A1)
        sibling(ox, y2)
    for row, oy in (("D", ym), ("U", yp)):
        go_wait(("+x", row + ",X2", "B0"), x2, oy, B0)
        go_wait(("-x", row + ",X2", "B1"), x2, oy, B1)
        sibling(x2, oy)
    z_round(8)
    go_wait(("+y", "X2,Y2", "A0"), x2, y2, A0)
    go_wait(("-y", "X2,Y2", "A1"), x2, y2, A1)
    go_wait(("+x", "Y2,X2", "B0"), x2, y2, B0)
    go_wait(("-x", "Y2,X2", "B1"), x2, y2, B1)
    sibling(x2, y2)
    for slot, (ox, oy) in enumerate(sib_slots):
        wait_in(gobuf.at[ox * 2 + 1 - k, oy], sib_r.at[slot])

    total = jnp.zeros((NY * ROWS, LANES), F32)
    for ox in range(NX):
        rel = (ox + NY - y) % NY
        for half in range(2):
            a = gobuf[ox * 2 + half].reshape(NY * ROWS, WIDE)
            w = wbuf[rel, half * 8 : half * 8 + 8].reshape(WIDE, LANES)
            total = total + jnp.dot(a, w, preferred_element_type=F32)
    gc[...] = total * gt[...].reshape(NY * ROWS, LANES).astype(F32)

    def start_step(i, sums):
        g = gc[pl.ds(SEG - 1 - i, 8, stride=SEG), :]
        return tuple(dec[m] * s + g for m, s in enumerate(sums))

    for m, s in enumerate(lax.fori_loop(0, SEG, start_step, zeros)):
        starts[m] = s

    def far_first():
        order = [8]
        for d in range(7, 0, -1):
            order += [d, NZ - d]
        return order

    arrived[z] = starts[z]
    for d in far_first():
        to = (z + d) % NZ
        send(starts.at[to], arrived.at[z], a_s.at[d], a_r.at[d], dev(dz=to))

    def near_step(i, carry):
        sums, inner = carry
        t = SEG - 1 - i
        g = gc[pl.ds(t, 8, stride=SEG), :]
        c = cvf[pl.ds(t, 8, stride=SEG), :]
        sums = tuple(dec[m] * s + g for m, s in enumerate(sums))
        inner = tuple(n + c * s for n, s in zip(inner, sums))
        acc = resb[0] * sums[0]
        for m in range(1, MODES):
            acc = acc + resb[m] * sums[m]
        near[t] = acc
        return sums, inner

    _, inner = lax.fori_loop(0, SEG, near_step, (zeros, zeros))
    for m in range(MODES):
        ends[m, 1] = inner[m]
    ends_in[z] = ends[z]
    for d in far_first():
        to = (z + d) % NZ
        send(ends.at[to], ends_in.at[z], e_s.at[d], e_r.at[d], dev(dz=to))

    for d in range(1, NZ):
        wait_in(arrived.at[(z + NZ - d) % NZ], a_r.at[d])
    rate = jnp.broadcast_to(rt[pl.ds(z, 1), :], (8, LANES))
    row = lax.broadcasted_iota(jnp.int32, (8, LANES), 0)
    even = row % 2 == 0
    by_seg = jnp.exp(-rate * F32(SEG))
    by_block = jnp.exp(-rate * F32(ROWS))
    by_line = jnp.exp(-rate * F32(ROWS * NZ))
    second, block = [], []
    for zz in range(NZ):
        s = arrived[zz]
        other = jnp.where(even, pltpu.roll(s, 7, 0), pltpu.roll(s, 1, 0))
        first = jnp.where(even, s, other)
        second.append(jnp.where(even, other, s))
        block.append(first + by_seg * second[zz])
    after = [None] * NZ
    after[NZ - 1] = jnp.zeros((8, LANES), F32)
    for zz in range(NZ - 2, -1, -1):
        after[zz] = block[zz + 1] + by_block * after[zz + 1]
    line = block[0] + by_block * after[0]

    def next_row(v):
        return jnp.where(row < 6, pltpu.roll(v, 6, 0), 0.0)

    line_next = next_row(line)
    lines = line_next
    for _ in range(2):
        lines = line_next + by_line * next_row(lines)
    ins = []
    for zz in range(NZ):
        late = after[zz] + jnp.exp(-rate * F32(ROWS * (NZ - 1 - zz))) * lines
        ins.append(jnp.where(even, second[zz] + by_seg * late, late))
        backs[zz] = ins[zz]
    incoming[z] = backs[z]
    for d in far_first():
        to = (z + d) % NZ
        send(backs.at[to], incoming.at[z], b_s.at[d], b_r.at[d], dev(dz=to))

    for d in range(1, NZ):
        wait_in(ends_in.at[(z + NZ - d) % NZ], e_r.at[d])
    grad = jnp.zeros((8, LANES), F32)
    for zz in range(NZ):
        grad = grad + (ends_in[zz, 1] + ends_in[zz, 0] * ins[zz])
    rowsum[...] = jnp.sum(grad, axis=0, keepdims=True) * F32(1.0 / LENGTH)
    rowsum_in[z] = rowsum[...]
    for d in far_first():
        to = (z + d) % NZ
        send(rowsum, rowsum_in.at[z], t_s.at[d], t_r.at[d], dev(dz=to))

    for d in range(1, NZ):
        wait_in(incoming.at[(z + NZ - d) % NZ], b_r.at[d])

    def far_step(i, sums):
        t = SEG - 1 - i
        sums = tuple(dec[m] * s for m, s in enumerate(sums))
        acc = near[t]
        for m in range(MODES):
            acc = acc + resb[m] * sums[m]
        outf[pl.ds(t, 8, stride=SEG), :] = acc
        return sums

    lax.fori_loop(0, SEG, far_step, tuple(incoming[m] for m in range(MODES)))
    for q in range(NY):
        outb[q] = outf[q * ROWS : (q + 1) * ROWS, :].astype(BF16)
    for r in (2, 1, 3):
        to = (y + r) % NY
        send(outb.at[to], out.at[:, cols], o_s.at[r], o_r.at[r], dev(dy=to))
    out[:, cols] = outb[y]

    for d in range(1, NZ):
        wait_in(rowsum_in.at[(z + NZ - d) % NZ], t_r.at[d])
    for m in range(MODES):
        rcomp[m : m + 1, :] = rowsum_in[m]
    for r in (2, 1, 3):
        to = (y + r) % NY
        send(rcomp, rout.at[:, cols], ro_s.at[r], ro_r.at[r], dev(dy=to))
    rout[:, cols] = rcomp[...]
    for r in range(1, NY):
        src = pl.ds(pl.multiple_of(((y + NY - r) % NY) * LANES, LANES), LANES)
        wait_in(out.at[:, src], o_r.at[r])
        wait_in(rout.at[:, src], ro_r.at[r])
    for c in unsent:
        c.wait_send()


def local(grad_out, gate, conv_input, out_weight, residues, rates):
    any_ = pl.BlockSpec(memory_space=pl.ANY)
    vmem = pl.BlockSpec(memory_space=pltpu.VMEM)
    dma = pltpu.SemaphoreType.DMA
    return pl.pallas_call(
        kernel,
        name="modal_backward",
        out_shape=(
            jax.ShapeDtypeStruct((ROWS, WIDE), BF16),
            jax.ShapeDtypeStruct((MODES, WIDE), F32),
        ),
        in_specs=[any_, any_, any_, vmem, any_, any_],
        out_specs=(vmem, vmem),
        scratch_shapes=[
            pltpu.VMEM((2 * NX, NY, ROWS, WIDE), BF16),
            pltpu.VMEM((NY, NZ, 64, LANES), BF16),
            pltpu.VMEM((NY, 64, LANES), BF16),
            pltpu.VMEM((NY, ROWS, LANES), BF16),
            pltpu.VMEM((NY, ROWS, LANES), BF16),
            pltpu.VMEM((MODES, LANES), F32),
            pltpu.VMEM((MODES, LANES), F32),
            pltpu.VMEM((MODES, 8, LANES), F32),
            pltpu.VMEM((MODES, 8, LANES), F32),
            pltpu.VMEM((NY * ROWS, LANES), F32),
            pltpu.VMEM((NY * ROWS, LANES), F32),
            pltpu.VMEM((SEG, 8, LANES), F32),
            pltpu.VMEM((MODES, 8, LANES), F32),
            pltpu.VMEM((NZ, 8, LANES), F32),
            pltpu.VMEM((MODES, 2, 8, LANES), F32),
            pltpu.VMEM((NZ, 2, 8, LANES), F32),
            pltpu.VMEM((NZ, 8, LANES), F32),
            pltpu.VMEM((MODES, 8, LANES), F32),
            pltpu.VMEM((1, LANES), F32),
            pltpu.VMEM((MODES, 1, LANES), F32),
            pltpu.VMEM((NY * ROWS, LANES), F32),
            pltpu.VMEM((NY, ROWS, LANES), BF16),
            pltpu.VMEM((MODES, LANES), F32),
            dma((5,)),
            dma((4,)), dma((4,)),
            dma((36,)), dma((36,)),
            dma((16,)), dma((16,)),
            dma((8,)), dma((8,)),
            dma((32,)), dma((32,)),
            dma((16,)), dma((16,)),
            dma((16,)), dma((16,)),
            dma((16,)), dma((16,)),
            dma((16,)), dma((16,)),
            dma((4,)), dma((4,)),
            dma((4,)), dma((4,)),
        ],
        compiler_params=pltpu.CompilerParams(
            collective_id=1, has_side_effects=True, vmem_limit_bytes=32 << 20
        ),
    )(grad_out, gate, conv_input, out_weight, residues, rates)


def solution(mesh):
    placed = (
        P("ctx", "tp"),
        P("ctx", "tp"),
        P("ctx", "tp"),
        P("tp", "ctx"),
        P(None, "tp"),
        P(None, "tp"),
    )
    return jax.shard_map(
        local,
        mesh=mesh,
        in_specs=placed,
        out_specs=(P("ctx", "tp"), P(None, "tp")),
        check_vma=False,
    )
```

time: 871 us -> 75.9 us (0.09)
  the two profiles are of different devices: /device:TPU:4 before, /device:TPU:1 now
where the time goes in v1:
time: 75.9 us; the launch traced here: 75.8 us
  Pallas kernels  71 us (94%)
  local copies, waits for them, and re-layouts  4.08 us (5%)
    pallas_call x1, Pallas kernels, local(): pl.pallas_call(kernel, name='modal_backward', out_shape=(jax.ShapeDtypeSt...  71 us
    unnamed x13, local copies, waits for them, and re-layouts  4.08 us

profile of v1, /device:TPU:1, one launch (start us, length us, event | category | flops | bytes accessed | tf_op | source)
XLA Modules:
  0.0 75.8 jit_solution(13278026651501358142)
XLA Ops:
  0.6 0.0 copy-start.4
  0.6 0.0 copy-start.3
  0.7 0.0 copy-start
  0.7 1.0 %copy.8.weight = bf16[512,64]{1,0:T(8,128)(2,1)S(1)} copy(bf16[512,64]{0,1:T(8,128)(2,1)} %param.9) | data formatting | bytes 131072 | tf_op args[3]
  1.7 0.0 copy-done.4
  1.7 0.0 copy-done.3
  1.7 0.0 copy-done
  1.7 0.0 copy-start.1
  1.7 0.9 %copy-done.1 = bf16[128,512]{1,0:T(8,128)(2,1)S(1)} copy-done((bf16[128,512]{1,0:T(8,128)(2,1)S(1)}, bf16[128,512]{1,0:T(8,128)(2,1)}, u32[]{:S(2)}) %copy-start.1) | copy-done | bytes 131096
  2.6 0.0 copy-start.2
  2.6 0.9 %copy-done.2 = bf16[128,512]{1,0:T(8,128)(2,1)S(1)} copy-done((bf16[128,512]{1,0:T(8,128)(2,1)S(1)}, bf16[128,512]{1,0:T(8,128)(2,1)}, u32[]{:S(2)}) %copy-start.2) | copy-done | bytes 131096
  3.5 71.0 %modal_backward.1 = (bf16[128,512]{1,0:T(8,128)(2,1)S(1)}, f32[16,512]{1,0:T(8,128)S(1)}) custom-call(bf16[128,512]{1,0:T(8,128)(2,1)S(1)} %copy-done, bf16[128,512]{1,0:T(8,128)(2,1)S(1)} %copy-done.1, bf16[128,512]{1,0:T(8,128)(2,1)S(1)} %copy-done.2, bf16[512,64]{1,0:T(8,128)(2,1)S(1)} %copy.8.weight, f32[16,512]{1,0:T(8,128)S(1)} %copy-done.3, ...), custom_call_target="tpu_custom_call" | custom-call | tf_op jit(solution)/shard_map/modal_backward/pallas_call | solution.py:393
  74.5 0.7 copy.11
  75.1 0.6 copy.12
Async XLA Ops:
  0.6 1.0 %copy-start.4 = (f32[16,512]{1,0:T(8,128)S(1)}, f32[16,512]{1,0:T(8,128)}, u32[]{:S(2)}) copy-start(f32[16,512]{1,0:T(8,128)} %rates.1) | copy-start | bytes 98308
  0.6 1.0 %copy-start.3 = (f32[16,512]{1,0:T(8,128)S(1)}, f32[16,512]{1,0:T(8,128)}, u32[]{:S(2)}) copy-start(f32[16,512]{1,0:T(8,128)} %residues.1) | copy-start | bytes 98308
  0.7 1.0 %copy-start = (bf16[128,512]{1,0:T(8,128)(2,1)S(1)}, bf16[128,512]{1,0:T(8,128)(2,1)}, u32[]{:S(2)}) copy-start(bf16[128,512]{1,0:T(8,128)(2,1)} %go.1) | copy-start | bytes 393220
  1.7 0.9 %copy-start.1 = (bf16[128,512]{1,0:T(8,128)(2,1)S(1)}, bf16[128,512]{1,0:T(8,128)(2,1)}, u32[]{:S(2)}) copy-start(bf16[128,512]{1,0:T(8,128)(2,1)} %gate.1) | copy-start | bytes 393220
  2.6 0.9 %copy-start.2 = (bf16[128,512]{1,0:T(8,128)(2,1)S(1)}, bf16[128,512]{1,0:T(8,128)(2,1)}, u32[]{:S(2)}) copy-start(bf16[128,512]{1,0:T(8,128)(2,1)} %conv.1) | copy-start | bytes 393220

commit v2 on v0

v2 whole, which is shorter than its diff:
```python
import jax
import jax.numpy as jnp
from jax import lax
from jax.experimental import pallas as pl
from jax.experimental.pallas import tpu as pltpu
from jax.sharding import PartitionSpec as P

MESH = pl.DeviceIdType.MESH
F32 = jnp.float32
BF16 = jnp.bfloat16
MODES = 16
NX = 4
NY = 4
NZ = 16
ROWS = 128
WIDE = 512
LANES = 128
SEG = 64
LENGTH = 8192


def kernel(
    go, gate, conv, weight, residues, rates,
    out, rout,
    gobuf, wbuf, gtcv, rt, rs, rt_all, rs_all,
    dec, resb, dec_all, resb_all, gc, cvf, nearf, near, starts, ends, sent, arrived, sent_end, arrived_end,
    inrow, inrow_in, backs, incoming, rowsum, rowsum_in, outf,
    loc_sem, go_s, go_r, sib_r, z_s, z_r, gc_s, gc_r,
    a_s, a_r, e_s, e_r, i_s, i_r, n_s, n_r, b_s, b_r, t_s, t_r,
):
    ctx = lax.axis_index("ctx")
    tp = lax.axis_index("tp")
    x, k = tp // 2, tp % 2
    y, z = ctx // NZ, ctx % NZ
    xp, xm, x2 = (x + 1) % NX, (x + 3) % NX, (x + 2) % NX
    yp, ym, y2 = (y + 1) % NY, (y + 3) % NY, (y + 2) % NY

    def up(n):
        return (z + NZ + n) % NZ

    def dev(dx=None, dy=None, dz=None, dk=None):
        xx = x if dx is None else dx
        yy = y if dy is None else dy
        zz = z if dz is None else dz
        kk = k if dk is None else dk
        return (yy * NZ + zz, xx * 2 + kk)

    near_devices = [dev(dx=xp), dev(dx=xm), dev(dx=x2), dev(dk=1 - k)]
    near_devices += [dev(dz=up(n)) for n in (1, -1, 2, -2)]
    for yy in (yp, ym, y2):
        near_devices += [dev(dy=yy, dz=up(n)) for n in (0, 2, -2)]
    barrier = pltpu.get_barrier_semaphore()
    for d in near_devices:
        pl.semaphore_signal(barrier, inc=1, device_id=d, device_id_type=MESH)

    def send(src, dst, ss, rs_, target):
        pltpu.make_async_remote_copy(
            src_ref=src, dst_ref=dst, send_sem=ss, recv_sem=rs_, device_id=target, device_id_type=MESH
        ).start()

    def wait(ref, sem):
        pltpu.make_async_copy(ref, ref, sem).wait()

    def lanes(i):
        return pl.ds(pl.multiple_of(i * LANES, LANES), LANES)

    def shard(ox, core, oy):
        return (ox * 2 + core) * NY + oy

    def piece(r, owner):
        return r * NZ + owner

    cols = lanes(y)
    locals_ = [
        pltpu.make_async_copy(go, gobuf.at[shard(x, k, y)], loc_sem.at[0]),
        pltpu.make_async_copy(gate.at[:, cols], gtcv.at[y], loc_sem.at[1]),
        pltpu.make_async_copy(conv.at[:, cols], gtcv.at[NY + y], loc_sem.at[2]),
        pltpu.make_async_copy(rates.at[:, cols], rt, loc_sem.at[3]),
        pltpu.make_async_copy(residues.at[:, cols], rs, loc_sem.at[4]),
        pltpu.make_async_copy(weight.at[:, cols], wbuf.at[piece(0, z)], loc_sem.at[5]),
        pltpu.make_async_copy(rates, rt_all, loc_sem.at[6]),
        pltpu.make_async_copy(residues, rs_all, loc_sem.at[7]),
    ]
    for c in locals_:
        c.start()

    pl.semaphore_wait(barrier, len(near_devices))

    def z_slot(way, r, far):
        return r * NZ + (far if way else NZ - far)

    def z_send(way, r, owner, far, hop, src=None, to=None):
        ref = wbuf.at[piece(r, owner)]
        target = dev(dy=to, dz=up(-hop if way else hop))
        send(ref if src is None else src, ref, z_s.at[0], z_r.at[z_slot(way, r, far)], target)

    def z_wait(way, r, far):
        wait(wbuf.at[piece(r, up(far if way else -far))], z_r.at[z_slot(way, r, far)])

    for r in (0, 1, 3, 2):
        to = (y + NY - r) % NY
        src = weight.at[:, lanes(to)]
        for hop in (2, 1) if r == 0 else (2,):
            for way in (0, 1):
                z_send(way, r, z, hop, hop, src, to)
    for r in (1, 3, 2):
        to = (y + NY - r) % NY
        send(weight.at[:, lanes(to)], wbuf.at[piece(r, z)], z_s.at[0], z_r.at[r * NZ], dev(dy=to))

    A, B = (0, 64), (64, 64)
    A0, A1, B0, B1 = (0, 32), (32, 32), (64, 32), (96, 32)
    go_slots = {}

    def go_ref(ox, oy, part):
        return gobuf.at[shard(ox, k, oy), pl.ds(part[0], part[1]), :]

    def go_send(key, ox, oy, part, target, src=None):
        slot = go_slots.setdefault(key, len(go_slots))
        ref = go_ref(ox, oy, part)
        send(ref if src is None else src, ref, go_s.at[0], go_r.at[slot], target)

    def go_wait(key, ox, oy, part):
        wait(go_ref(ox, oy, part), go_r.at[go_slots[key]])

    one_way = (("L", dev(dx=xp)), ("R", dev(dx=xm)), ("X2", dev(dx=x2)))
    other_way = (("D", dev(dy=yp)), ("U", dev(dy=ym)), ("Y2", dev(dy=y2)))
    for near_part, far_part in ((A, B), (B, A)):
        for way, part in ((one_way, near_part), (other_way, far_part)):
            for key, target in way:
                go_send((key, part), x, y, part, target, go.at[pl.ds(part[0], part[1]), :])

    sib_slots = []

    def sibling(ox, oy, src=None):
        ref = gobuf.at[shard(ox, k, oy)]
        send(ref if src is None else src, ref, go_s.at[0], sib_r.at[0], dev(dk=1 - k))
        sib_slots.append((ox, oy))

    sibling(x, y, go)

    def z_round(far):
        for r in (0, 1, 3, 2):
            for way in (0, 1):
                owner = up(far if way else -far)
                z_wait(way, r, far)
                if far < 6 or way == r % 2:
                    z_send(way, r, owner, far + 2, 2)
                z_send(way, r, owner, far + 1, 1)

    for r in (1, 3, 2):
        wait(wbuf.at[piece(r, z)], z_r.at[r * NZ])
        for way in (0, 1):
            z_send(way, r, z, 1, 1)
    z_round(2)
    for r in range(1, NY):
        to = (y + r) % NY
        send(gate.at[:, lanes(to)], gtcv.at[y], gc_s.at[0], gc_r.at[0], dev(dy=to))
        send(conv.at[:, lanes(to)], gtcv.at[NY + y], gc_s.at[0], gc_r.at[0], dev(dy=to))
    columns = (("L", xm), ("R", xp), ("X2", x2))
    lines_ = (("D", ym), ("U", yp), ("Y2", y2))

    def turn(i):
        key, ox = columns[i]
        go_wait((key, A), ox, y, A)
        go_send((key, "D"), ox, y, A, dev(dy=yp))
        go_send((key, "U"), ox, y, A, dev(dy=ym))
        key, oy = lines_[i]
        go_wait((key, B), x, oy, B)
        go_send((key, "L"), x, oy, B, dev(dx=xp))
        go_send((key, "R"), x, oy, B, dev(dx=xm))

    def onward(i):
        key, ox = columns[i]
        go_wait((key, "D"), ox, ym, A)
        go_send((key, "Y2"), ox, ym, A0, dev(dy=yp))
        go_wait((key, "U"), ox, yp, A)
        go_send((key, "Y2"), ox, yp, A1, dev(dy=ym))
        key, oy = lines_[i]
        go_wait((key, "L"), xm, oy, B)
        go_send((key, "X2"), xm, oy, B0, dev(dx=xp))
        go_wait((key, "R"), xp, oy, B)
        go_send((key, "X2"), xp, oy, B1, dev(dx=xm))

    turn(0)
    turn(1)
    turn(2)
    for c in locals_:
        c.wait()
    for m in range(MODES):
        dec[m] = jnp.broadcast_to(jnp.exp(-rt[m : m + 1, :]), (8, LANES))
        resb[m] = jnp.broadcast_to(rs[m : m + 1, :], (8, LANES))
    z_round(4)
    for i in range(3):
        key, ox = columns[i]
        go_wait((key, B), ox, y, B)
        sibling(ox, y)
        key, oy = lines_[i]
        go_wait((key, A), x, oy, A)
        sibling(x, oy)
    onward(0)
    onward(1)
    for ox in (xm, xp):
        for oy in (ym, yp):
            sibling(ox, oy)

    def spread(ref, m):
        rows = [jnp.broadcast_to(ref[m : m + 1, q * LANES : (q + 1) * LANES], (2, LANES)) for q in range(NY)]
        return jnp.concatenate(rows, axis=0)

    for m in range(MODES):
        dec_all[m] = jnp.exp(-spread(rt_all, m))
        resb_all[m] = spread(rs_all, m)
    z_round(6)
    onward(2)
    wait(gtcv.at[pl.ds(0, 6)], gc_r.at[0])
    cvf[...] = gtcv[NY : 2 * NY].reshape(NY * ROWS, LANES).astype(F32)

    def end_step(t, sums):
        c = cvf[pl.ds(t, 8, stride=SEG), :]
        return tuple(dec[m] * (s + c) for m, s in enumerate(sums))

    zeros = tuple(jnp.zeros((8, LANES), F32) for _ in range(MODES))
    for m, s in enumerate(lax.fori_loop(0, SEG, end_step, zeros)):
        ends[m] = s
    for i in range(2):
        key, ox = columns[i]
        go_wait((key, "Y2"), ox, y2, A)
        sibling(ox, y2)
        key, oy = lines_[i]
        go_wait((key, "X2"), x2, oy, B)
        sibling(x2, oy)
    go_wait(("X2", "Y2"), x2, y2, A)
    go_wait(("Y2", "X2"), x2, y2, B)
    sibling(x2, y2)
    for far in (1, 3, 5, 7, 8):
        for r in range(NY):
            for way in (0, 1):
                if far < 8 or way == r % 2:
                    z_wait(way, r, far)
    wait(gobuf.at[pl.ds(0, NX * NY)], sib_r.at[0])

    total = jnp.zeros((NY * ROWS, LANES), F32)
    for ox in range(NX):
        rel = (ox + NY - y) % NY
        for half in range(2):
            a = gobuf[(ox * 2 + half) * NY : (ox * 2 + half + 1) * NY].reshape(NY * ROWS, WIDE)
            w = wbuf[pl.ds(rel * NZ + half * 8, 8)].reshape(WIDE, LANES)
            total = total + jnp.dot(a, w, preferred_element_type=F32)
    gc[...] = total * gtcv[:NY].reshape(NY * ROWS, LANES).astype(F32)

    def start_step(i, sums):
        g = gc[pl.ds(SEG - 1 - i, 8, stride=SEG), :]
        return tuple(dec[m] * s + g for m, s in enumerate(sums))

    row = lax.broadcasted_iota(jnp.int32, (8, LANES), 0)
    even = row % 2 == 0

    def by_seg(m):
        return jnp.broadcast_to(jnp.exp(-rt[m : m + 1, :] * F32(SEG)), (8, LANES))

    def next_up(v):
        return pltpu.roll(v, 7, 0)

    def next_down(v):
        return pltpu.roll(v, 1, 0)

    half_modes = MODES // 2
    sums = lax.fori_loop(0, SEG, start_step, zeros)
    for p in range(half_modes):
        s, o = sums[p], sums[p + half_modes]
        sent[p] = jnp.where(even, s + by_seg(p) * next_up(s), next_down(o) + by_seg(p + half_modes) * o)

    far_first = [8]
    for d in range(7, 0, -1):
        far_first += [d, -d]

    arrived[z] = sent[z % half_modes]
    for d in far_first:
        send(sent.at[up(d) % half_modes], arrived.at[z], a_s.at[0], a_r.at[0], dev(dz=up(d)))
    for p in range(half_modes):
        s, o = ends[p], ends[p + half_modes]
        sent_end[p] = jnp.where(even, next_up(s) + by_seg(p) * s, o + by_seg(p + half_modes) * next_down(o))
    arrived_end[z] = sent_end[z % half_modes]
    for d in far_first:
        send(sent_end.at[up(d) % half_modes], arrived_end.at[z], e_s.at[0], e_r.at[0], dev(dz=up(d)))

    def near_step(i, carry):
        sums, inner = carry
        t = SEG - 1 - i
        g = gc[pl.ds(t, 8, stride=SEG), :]
        c = cvf[pl.ds(t, 8, stride=SEG), :]
        sums = tuple(dec[m] * s + g for m, s in enumerate(sums))
        inner = tuple(n + c * s for n, s in zip(inner, sums))
        acc = resb[0] * sums[0]
        for m in range(1, MODES):
            acc = acc + resb[m] * sums[m]
        nearf[pl.ds(t, 8, stride=SEG), :] = acc
        return sums, inner

    from_second = tuple(jnp.where(even, next_up(s), 0.0) for s in sums)
    _, inner = lax.fori_loop(0, SEG, near_step, (from_second, zeros))
    for m in range(MODES):
        inrow[m % half_modes, m // half_modes : m // half_modes + 1, :] = jnp.sum(inner[m], axis=0, keepdims=True)
    inrow_in[z] = inrow[z % half_modes]
    for d in far_first:
        send(inrow.at[up(d) % half_modes], inrow_in.at[z], i_s.at[0], i_r.at[0], dev(dz=up(d)))
    for r in (2, 1, 3):
        to = (y + r) % NY
        rows = pl.ds(pl.multiple_of(to * ROWS, ROWS), ROWS)
        mine = pl.ds(pl.multiple_of(y * ROWS, ROWS), ROWS)
        send(nearf.at[rows, :], near.at[mine, :], n_s.at[0], n_r.at[0], dev(dy=to))
    near[mine, :] = nearf[mine, :]

    pair = z % half_modes
    rate = jnp.where(even, rt[pl.ds(pair, 1), :], rt[pl.ds(pair + half_modes, 1), :])
    by_block = jnp.exp(-rate * F32(ROWS))
    by_line = jnp.exp(-rate * F32(ROWS * NZ))
    to_line = [jnp.exp(-rate * F32(ROWS * (NZ - 1 - zz))) for zz in range(NZ)]
    wait(arrived.at[pl.ds(0, NZ - 1)], a_r.at[0])
    after = [None] * NZ
    after[NZ - 1] = jnp.zeros((8, LANES), F32)
    for zz in range(NZ - 2, -1, -1):
        after[zz] = arrived[zz + 1] + by_block * after[zz + 1]
    line = arrived[0] + by_block * after[0]

    def next_line(v):
        return jnp.where(row < 6, pltpu.roll(v, 6, 0), 0.0)

    line_next = next_line(line)
    lines = line_next
    for _ in range(NY - 2):
        lines = line_next + by_line * next_line(lines)
    ins = []
    for zz in range(NZ):
        ins.append(after[zz] + to_line[zz] * lines)
        for b in range(NY):
            backs[zz * NY + b] = ins[zz][2 * b : 2 * b + 2]

    served = (-4, 3, -3, 2, -2, 1, -1, 0)
    slot = pair * NY + y
    incoming[slot] = backs[z * NY + y]
    for d in served:
        for r in (2, 1, 3, 0):
            if d or r:
                to = (y + r) % NY
                send(backs.at[up(d) * NY + to], incoming.at[slot], b_s.at[0], b_r.at[0], dev(dy=to, dz=up(d)))

    wait(arrived_end.at[pl.ds(0, NZ - 1)], e_r.at[0])
    grad = jnp.zeros((8, LANES), F32)
    for zz in range(NZ):
        grad = grad + arrived_end[zz] * ins[zz]
    grad = grad + pltpu.roll(grad, 4, 0)
    grad = (grad + pltpu.roll(grad, 2, 0))[:2]
    wait(inrow_in.at[pl.ds(0, NZ - 1)], i_r.at[0])
    for zz in range(NZ):
        grad = grad + inrow_in[zz]
    rowsum[...] = grad * F32(1.0 / LENGTH)
    rowsum_in[slot] = rowsum[...]
    for d in served:
        for r in (2, 1, 3, 0):
            if d or r:
                to = (y + r) % NY
                send(rowsum, rowsum_in.at[slot], t_s.at[0], t_r.at[0], dev(dy=to, dz=up(d)))

    wait(near.at[pl.ds(0, 3 * ROWS), :], n_r.at[0])
    wait(incoming.at[pl.ds(0, half_modes * NY - 1)], b_r.at[0])
    carried = [None] * MODES
    for p in range(half_modes):
        both = jnp.concatenate([incoming[p * NY + q] for q in range(NY)], axis=0)
        for m, late in (
            (p, jnp.where(even, both, next_down(both))),
            (p + half_modes, jnp.where(even, next_up(both), both)),
        ):
            carried[m] = jnp.where(even, jnp.exp(-spread(rt_all, m) * F32(SEG)) * late, late)

    def far_step(i, sums):
        t = SEG - 1 - i
        sums = tuple(dec_all[m] * s for m, s in enumerate(sums))
        acc = near[pl.ds(t, 8, stride=SEG), :]
        for m in range(MODES):
            acc = acc + resb_all[m] * sums[m]
        outf[pl.ds(t, 8, stride=SEG), :] = acc
        return sums

    lax.fori_loop(0, SEG, far_step, tuple(carried))
    for q in range(NY):
        out[:, q * LANES : (q + 1) * LANES] = outf[q * ROWS : (q + 1) * ROWS, :].astype(BF16)

    wait(rowsum_in.at[pl.ds(0, half_modes * NY - 1)], t_r.at[0])
    for m in range(MODES):
        for q in range(NY):
            j = m // half_modes
            rout[m : m + 1, q * LANES : (q + 1) * LANES] = rowsum_in[(m % half_modes) * NY + q, j : j + 1, :]

    wait(gobuf.at[pl.ds(0, 31)], go_s.at[0])
    wait(wbuf.at[pl.ds(0, 63)], z_s.at[0])
    wait(gtcv.at[pl.ds(0, 6)], gc_s.at[0])
    wait(arrived.at[pl.ds(0, NZ - 1)], a_s.at[0])
    wait(arrived.at[pl.ds(0, NZ - 1)], e_s.at[0])
    wait(inrow_in.at[pl.ds(0, NZ - 1)], i_s.at[0])
    wait(near.at[pl.ds(0, 3 * ROWS), :], n_s.at[0])
    wait(incoming.at[pl.ds(0, 31)], b_s.at[0])
    wait(incoming.at[pl.ds(0, 31)], t_s.at[0])


def local(grad_out, gate, conv_input, out_weight, residues, rates):
    hbm = pl.BlockSpec(memory_space=pltpu.HBM)
    vmem = pl.BlockSpec(memory_space=pltpu.VMEM)
    dma = pltpu.SemaphoreType.DMA

    def f32(*shape):
        return pltpu.VMEM(shape, F32)

    def bf16(*shape):
        return pltpu.VMEM(shape, BF16)

    return pl.pallas_call(
        kernel,
        name="modal_backward",
        out_shape=(
            jax.ShapeDtypeStruct((ROWS, WIDE), BF16),
            jax.ShapeDtypeStruct((MODES, WIDE), F32),
        ),
        in_specs=[hbm] * 6,
        out_specs=(vmem, vmem),
        scratch_shapes=[
            bf16(2 * NX * NY, ROWS, WIDE),
            bf16(NY * NZ, 64, LANES),
            bf16(2 * NY, ROWS, LANES),
            f32(MODES, LANES),
            f32(MODES, LANES),
            f32(MODES, WIDE),
            f32(MODES, WIDE),
            f32(MODES, 8, LANES),
            f32(MODES, 8, LANES),
            f32(MODES, 8, LANES),
            f32(MODES, 8, LANES),
            f32(NY * ROWS, LANES),
            f32(NY * ROWS, LANES),
            f32(NY * ROWS, LANES),
            f32(NY * ROWS, LANES),
            f32(MODES, 8, LANES),
            f32(MODES, 8, LANES),
            f32(MODES // 2, 8, LANES),
            f32(NZ, 8, LANES),
            f32(MODES // 2, 8, LANES),
            f32(NZ, 8, LANES),
            f32(MODES // 2, 2, LANES),
            f32(NZ, 2, LANES),
            f32(NZ * NY, 2, LANES),
            f32(MODES // 2 * NY, 2, LANES),
            f32(2, LANES),
            f32(MODES // 2 * NY, 2, LANES),
            f32(NY * ROWS, LANES),
            dma((8,)),
            dma((1,)), dma((30,)), dma((1,)),
            dma((1,)), dma((NY * NZ,)),
            dma((1,)), dma((1,)),
            dma((1,)), dma((1,)),
            dma((1,)), dma((1,)),
            dma((1,)), dma((1,)),
            dma((1,)), dma((1,)),
            dma((1,)), dma((1,)),
            dma((1,)), dma((1,)),
        ],
        compiler_params=pltpu.CompilerParams(
            collective_id=1, has_side_effects=True, vmem_limit_bytes=63 << 20
        ),
    )(grad_out, gate, conv_input, out_weight.T, residues, rates)


def solution(mesh):
    placed = (
        P("ctx", "tp"),
        P("ctx", "tp"),
        P("ctx", "tp"),
        P("tp", "ctx"),
        P(None, "tp"),
        P(None, "tp"),
    )
    return jax.shard_map(
        local,
        mesh=mesh,
        in_specs=placed,
        out_specs=(P("ctx", "tp"), P(None, "tp")),
        check_vma=False,
    )
```

time: 871 us -> 61.9 us (0.07)
  the two profiles are of different devices: /device:TPU:4 before, /device:TPU:1 now
where the time goes in v2:
time: 61.9 us; the launch traced here: 61.8 us
  Pallas kernels  58.9 us (95%)
  local copies, waits for them, and re-layouts  2.19 us (4%)
  between operations  0.65 us (1%)
    pallas_call x1, Pallas kernels, local(): pl.pallas_call(kernel, name='modal_backward', out_shape=(jax.ShapeDtypeSt...  58.9 us
    unnamed x4, local copies, waits for them, and re-layouts  2.19 us

profile of v2, /device:TPU:1, one launch (start us, length us, event | category | flops | bytes accessed | tf_op | source)
XLA Modules:
  0.0 61.8 jit_solution(17268995036442498121)
XLA Ops:
  0.6 58.9 %modal_backward.1 = (bf16[128,512]{1,0:T(8,128)(2,1)}, f32[16,512]{1,0:T(8,128)}) custom-call(bf16[128,512]{1,0:T(8,128)(2,1)} %go.1, bf16[128,512]{1,0:T(8,128)(2,1)} %gate.1, bf16[128,512]{1,0:T(8,128)(2,1)} %conv.1, bf16[64,512]{1,0:T(8,128)(2,1)} %bitcast.1, f32[16,512]{1,0:T(8,128)} %residues.1, f32[16,512]{1,0:T(8,128)} %rates.1), custom_call_target="tpu_custom_call" | custom-call | tf_op jit(solution)/shard_map/modal_backward/pallas_call | solution.py:417
  59.6 0.0 copy-start
  59.6 1.6 %copy.10 = bf16[128,512]{1,0:T(8,128)(2,1)} copy(bf16[128,512]{1,0:T(8,128)(2,1)} %get-tuple-element.4) | data formatting | bytes 262144
  61.2 0.0 copy-done
  61.2 0.6 copy.11
Async XLA Ops:
  59.6 1.6 %copy-start = (f32[16,512]{1,0:T(8,128)S(1)}, f32[16,512]{1,0:T(8,128)}, u32[]{:S(2)}) copy-start(f32[16,512]{1,0:T(8,128)} %get-tuple-element.5) | copy-start | bytes 98308

commit v3 on v2

--- a/solution.py
+++ b/solution.py
@@ -17,13 +17,14 @@
 LANES = 128
 SEG = 64
 LENGTH = 8192
+HOPS = {0: (2, 1), 2: (2, 1), 4: (2, 1), 6: (2, 1)}
 
 
 def kernel(
     go, gate, conv, weight, residues, rates,
     out, rout,
     gobuf, wbuf, gtcv, rt, rs, rt_all, rs_all,
-    dec, resb, dec_all, resb_all, gc, cvf, nearf, near, starts, ends, sent, arrived, sent_end, arrived_end,
+    dec, resb, dec_all, resb_all, seg_all, gc, cvf, nearf, near, sent, arrived, sent_end, arrived_end,
     inrow, inrow_in, backs, incoming, rowsum, rowsum_in, outf,
     loc_sem, go_s, go_r, sib_r, z_s, z_r, gc_s, gc_r,
     a_s, a_r, e_s, e_r, i_s, i_r, n_s, n_r, b_s, b_r, t_s, t_r,
@@ -100,15 +101,15 @@
     for r in (0, 1, 3, 2):
         to = (y + NY - r) % NY
         src = weight.at[:, lanes(to)]
-        for hop in (2, 1) if r == 0 else (2,):
+        for hop in HOPS[0] if r == 0 else HOPS[0][:1]:
             for way in (0, 1):
                 z_send(way, r, z, hop, hop, src, to)
     for r in (1, 3, 2):
         to = (y + NY - r) % NY
         send(weight.at[:, lanes(to)], wbuf.at[piece(r, z)], z_s.at[0], z_r.at[r * NZ], dev(dy=to))
 
-    A, B = (0, 64), (64, 64)
-    A0, A1, B0, B1 = (0, 32), (32, 32), (64, 32), (96, 32)
+    A, B = (0, 48), (48, 80)
+    A0, A1, B0, B1 = (0, 32), (32, 16), (48, 48), (96, 32)
     go_slots = {}
 
     def go_ref(ox, oy, part):
@@ -138,24 +139,21 @@
 
     sibling(x, y, go)
 
-    def z_round(far):
-        for r in (0, 1, 3, 2):
+    def z_round(far, pieces=(0, 1, 3, 2)):
+        for r in pieces:
             for way in (0, 1):
                 owner = up(far if way else -far)
                 z_wait(way, r, far)
-                if far < 6 or way == r % 2:
-                    z_send(way, r, owner, far + 2, 2)
-                z_send(way, r, owner, far + 1, 1)
-
-    for r in (1, 3, 2):
-        wait(wbuf.at[piece(r, z)], z_r.at[r * NZ])
-        for way in (0, 1):
-            z_send(way, r, z, 1, 1)
-    z_round(2)
-    for r in range(1, NY):
-        to = (y + r) % NY
-        send(gate.at[:, lanes(to)], gtcv.at[y], gc_s.at[0], gc_r.at[0], dev(dy=to))
-        send(conv.at[:, lanes(to)], gtcv.at[NY + y], gc_s.at[0], gc_r.at[0], dev(dy=to))
+                for hop in HOPS[far]:
+                    if far + hop < 8 or way == r % 2:
+                        z_send(way, r, owner, far + hop, hop)
+
+    def y_pieces():
+        for r in (1, 3, 2):
+            wait(wbuf.at[piece(r, z)], z_r.at[r * NZ])
+            for way in (0, 1):
+                z_send(way, r, z, 1, 1)
+
     columns = (("L", xm), ("R", xp), ("X2", x2))
     lines_ = (("D", ym), ("U", yp), ("Y2", y2))
 
@@ -181,62 +179,119 @@
         go_wait((key, "R"), xp, oy, B)
         go_send((key, "X2"), xp, oy, B1, dev(dx=xm))
 
-    turn(0)
-    turn(1)
-    turn(2)
-    for c in locals_:
-        c.wait()
-    for m in range(MODES):
-        dec[m] = jnp.broadcast_to(jnp.exp(-rt[m : m + 1, :]), (8, LANES))
-        resb[m] = jnp.broadcast_to(rs[m : m + 1, :], (8, LANES))
-    z_round(4)
-    for i in range(3):
+    def gates():
+        for r in range(1, NY):
+            to = (y + r) % NY
+            send(gate.at[:, lanes(to)], gtcv.at[y], gc_s.at[0], gc_r.at[0], dev(dy=to))
+            send(conv.at[:, lanes(to)], gtcv.at[NY + y], gc_s.at[0], gc_r.at[0], dev(dy=to))
+
+    def near_shards(i):
         key, ox = columns[i]
         go_wait((key, B), ox, y, B)
         sibling(ox, y)
         key, oy = lines_[i]
         go_wait((key, A), x, oy, A)
         sibling(x, oy)
-    onward(0)
-    onward(1)
-    for ox in (xm, xp):
-        for oy in (ym, yp):
-            sibling(ox, oy)
+
+    def diagonal_shards():
+        for ox in (xm, xp):
+            for oy in (ym, yp):
+                sibling(ox, oy)
+
+    def far_shards(i):
+        key, ox = columns[i]
+        go_wait((key, "Y2"), ox, y2, A)
+        if i < 2:
+            sibling(ox, y2)
+        key, oy = lines_[i]
+        go_wait((key, "X2"), x2, oy, B)
+        sibling(x2, oy)
 
     def spread(ref, m):
         rows = [jnp.broadcast_to(ref[m : m + 1, q * LANES : (q + 1) * LANES], (2, LANES)) for q in range(NY)]
         return jnp.concatenate(rows, axis=0)
 
-    for m in range(MODES):
-        dec_all[m] = jnp.exp(-spread(rt_all, m))
-        resb_all[m] = spread(rs_all, m)
-    z_round(6)
-    onward(2)
-    wait(gtcv.at[pl.ds(0, 6)], gc_r.at[0])
-    cvf[...] = gtcv[NY : 2 * NY].reshape(NY * ROWS, LANES).astype(F32)
+    def decays():
+        for c in locals_:
+            c.wait()
+        for m in range(MODES):
+            dec[m] = jnp.broadcast_to(jnp.exp(-rt[m : m + 1, :]), (8, LANES))
+            resb[m] = jnp.broadcast_to(rs[m : m + 1, :], (8, LANES))
+            rate = spread(rt_all, m)
+            dec_all[m] = jnp.exp(-rate)
+            seg_all[m] = jnp.exp(-rate * F32(SEG))
+            resb_all[m] = spread(rs_all, m)
+
+    row = lax.broadcasted_iota(jnp.int32, (8, LANES), 0)
+    even = row % 2 == 0
+
+    def by_seg(m):
+        return jnp.broadcast_to(jnp.exp(-rt[m : m + 1, :] * F32(SEG)), (8, LANES))
+
+    def next_up(v):
+        return pltpu.roll(v, 7, 0)
+
+    def next_down(v):
+        return pltpu.roll(v, 1, 0)
+
+    half_modes = MODES // 2
+    far_first = [8]
+    for d in range(7, 0, -1):
+        far_first += [d, -d]
+
+    zeros = tuple(jnp.zeros((8, LANES), F32) for _ in range(MODES))
 
     def end_step(t, sums):
         c = cvf[pl.ds(t, 8, stride=SEG), :]
         return tuple(dec[m] * (s + c) for m, s in enumerate(sums))
 
-    zeros = tuple(jnp.zeros((8, LANES), F32) for _ in range(MODES))
-    for m, s in enumerate(lax.fori_loop(0, SEG, end_step, zeros)):
-        ends[m] = s
-    for i in range(2):
-        key, ox = columns[i]
-        go_wait((key, "Y2"), ox, y2, A)
-        sibling(ox, y2)
-        key, oy = lines_[i]
-        go_wait((key, "X2"), x2, oy, B)
-        sibling(x2, oy)
-    go_wait(("X2", "Y2"), x2, y2, A)
-    go_wait(("Y2", "X2"), x2, y2, B)
-    sibling(x2, y2)
-    for far in (1, 3, 5, 7, 8):
-        for r in range(NY):
-            for way in (0, 1):
-                if far < 8 or way == r % 2:
-                    z_wait(way, r, far)
+    def input_ends():
+        wait(gtcv.at[pl.ds(0, 6)], gc_r.at[0])
+        cvf[...] = gtcv[NY : 2 * NY].reshape(NY * ROWS, LANES).astype(F32)
+        sums = lax.fori_loop(0, SEG, end_step, zeros)
+        for p in range(half_modes):
+            s, o = sums[p], sums[p + half_modes]
+            sent_end[p] = jnp.where(even, next_up(s) + by_seg(p) * s, o + by_seg(p + half_modes) * next_down(o))
+        arrived_end[z] = sent_end[z % half_modes]
+
+    def send_ends(chips):
+        for d in chips:
+            send(sent_end.at[up(d) % half_modes], arrived_end.at[z], e_s.at[0], e_r.at[0], dev(dz=up(d)))
+
+    def z_leaves(fars):
+        for far in fars:
+            for r in range(NY):
+                for way in (0, 1):
+                    if far < 8 or way == r % 2:
+                        z_wait(way, r, far)
+
+    z_round(2, (0,))
+    turn(0)
+    turn(1)
+    z_round(2, (1, 3, 2))
+    y_pieces()
+    turn(2)
+    gates()
+    decays()
+    near_shards(0)
+    near_shards(1)
+    near_shards(2)
+    z_round(4, (0, 1))
+    onward(0)
+    z_round(4, (3, 2))
+    onward(1)
+    diagonal_shards()
+    onward(2)
+    input_ends()
+    z_round(6, (0, 1))
+    far_shards(0)
+    z_round(6, (3, 2))
+    z_leaves((1, 3, 5))
+    send_ends((6, -6, 5, -5, 4, -4, 3, -3, 2, -2, 1, -1))
+    far_shards(1)
+    far_shards(2)
+    z_leaves((7, 8))
+    send_ends((8, 7, -7))
     wait(gobuf.at[pl.ds(0, NX * NY)], sib_r.at[0])
 
     total = jnp.zeros((NY * ROWS, LANES), F32)
@@ -252,58 +307,40 @@
         g = gc[pl.ds(SEG - 1 - i, 8, stride=SEG), :]
         return tuple(dec[m] * s + g for m, s in enumerate(sums))
 
-    row = lax.broadcasted_iota(jnp.int32, (8, LANES), 0)
-    even = row % 2 == 0
-
-    def by_seg(m):
-        return jnp.broadcast_to(jnp.exp(-rt[m : m + 1, :] * F32(SEG)), (8, LANES))
-
-    def next_up(v):
-        return pltpu.roll(v, 7, 0)
-
-    def next_down(v):
-        return pltpu.roll(v, 1, 0)
-
-    half_modes = MODES // 2
     sums = lax.fori_loop(0, SEG, start_step, zeros)
     for p in range(half_modes):
         s, o = sums[p], sums[p + half_modes]
         sent[p] = jnp.where(even, s + by_seg(p) * next_up(s), next_down(o) + by_seg(p + half_modes) * o)
 
-    far_first = [8]
-    for d in range(7, 0, -1):
-        far_first += [d, -d]
-
     arrived[z] = sent[z % half_modes]
     for d in far_first:
         send(sent.at[up(d) % half_modes], arrived.at[z], a_s.at[0], a_r.at[0], dev(dz=up(d)))
-    for p in range(half_modes):
-        s, o = ends[p], ends[p + half_modes]
-        sent_end[p] = jnp.where(even, next_up(s) + by_seg(p) * s, o + by_seg(p + half_modes) * next_down(o))
-    arrived_end[z] = sent_end[z % half_modes]
-    for d in far_first:
-        send(sent_end.at[up(d) % half_modes], arrived_end.at[z], e_s.at[0], e_r.at[0], dev(dz=up(d)))
-
-    def near_step(i, carry):
+    def inner_step(i, carry):
         sums, inner = carry
-        t = SEG - 1 - i
-        g = gc[pl.ds(t, 8, stride=SEG), :]
-        c = cvf[pl.ds(t, 8, stride=SEG), :]
+        g = gc[pl.ds(SEG - 1 - i, 8, stride=SEG), :]
+        c = cvf[pl.ds(SEG - 1 - i, 8, stride=SEG), :]
         sums = tuple(dec[m] * s + g for m, s in enumerate(sums))
-        inner = tuple(n + c * s for n, s in zip(inner, sums))
-        acc = resb[0] * sums[0]
-        for m in range(1, MODES):
-            acc = acc + resb[m] * sums[m]
-        nearf[pl.ds(t, 8, stride=SEG), :] = acc
-        return sums, inner
+        return sums, tuple(n + c * s for n, s in zip(inner, sums))
 
     from_second = tuple(jnp.where(even, next_up(s), 0.0) for s in sums)
-    _, inner = lax.fori_loop(0, SEG, near_step, (from_second, zeros))
+    _, inner = lax.fori_loop(0, SEG, inner_step, (from_second, zeros))
     for m in range(MODES):
         inrow[m % half_modes, m // half_modes : m // half_modes + 1, :] = jnp.sum(inner[m], axis=0, keepdims=True)
     inrow_in[z] = inrow[z % half_modes]
     for d in far_first:
         send(inrow.at[up(d) % half_modes], inrow_in.at[z], i_s.at[0], i_r.at[0], dev(dz=up(d)))
+
+    def near_step(i, sums):
+        t = SEG - 1 - i
+        g = gc[pl.ds(t, 8, stride=SEG), :]
+        sums = tuple(dec[m] * s + g for m, s in enumerate(sums))
+        acc = resb[0] * sums[0]
+        for m in range(1, MODES):
+            acc = acc + resb[m] * sums[m]
+        nearf[pl.ds(t, 8, stride=SEG), :] = acc
+        return sums
+
+    lax.fori_loop(0, SEG, near_step, from_second)
     for r in (2, 1, 3):
         to = (y + r) % NY
         rows = pl.ds(pl.multiple_of(to * ROWS, ROWS), ROWS)
@@ -371,7 +408,7 @@
             (p, jnp.where(even, both, next_down(both))),
             (p + half_modes, jnp.where(even, next_up(both), both)),
         ):
-            carried[m] = jnp.where(even, jnp.exp(-spread(rt_all, m) * F32(SEG)) * late, late)
+            carried[m] = jnp.where(even, seg_all[m] * late, late)
 
     def far_step(i, sums):
         t = SEG - 1 - i
@@ -414,6 +451,8 @@
     def bf16(*shape):
         return pltpu.VMEM(shape, BF16)
 
+    operands = (grad_out, gate, conv_input, out_weight.T, residues, rates)
+    operands = [pltpu.with_memory_space_constraint(a, pltpu.HBM) for a in operands]
     return pl.pallas_call(
         kernel,
         name="modal_backward",
@@ -435,12 +474,11 @@
             f32(MODES, 8, LANES),
             f32(MODES, 8, LANES),
             f32(MODES, 8, LANES),
+            f32(MODES, 8, LANES),
             f32(NY * ROWS, LANES),
             f32(NY * ROWS, LANES),
             f32(NY * ROWS, LANES),
             f32(NY * ROWS, LANES),
-            f32(MODES, 8, LANES),
-            f32(MODES, 8, LANES),
             f32(MODES // 2, 8, LANES),
             f32(NZ, 8, LANES),
             f32(MODES // 2, 8, LANES),
@@ -464,9 +502,9 @@
             dma((1,)), dma((1,)),
         ],
         compiler_params=pltpu.CompilerParams(
-            collective_id=1, has_side_effects=True, vmem_limit_bytes=63 << 20
+            collective_id=1, has_side_effects=True, vmem_limit_bytes=32 << 20
         ),
-    )(grad_out, gate, conv_input, out_weight.T, residues, rates)
+    )(*operands)
 
 
 def solution(mesh):

time: 61.9 us -> 57.2 us (0.924)
  the two profiles are of different devices: /device:TPU:1 before, /device:TPU:2 now
where the time goes in v3:
time: 57.2 us; the launch traced here: 57.1 us
  Pallas kernels  55.2 us (97%)
  local copies, waits for them, and re-layouts  1.27 us (2%)
  between operations  0.64 us (1%)
    pallas_call x1, Pallas kernels, local(): pl.pallas_call(kernel, name='modal_backward', out_shape=(jax.ShapeDtypeSt...  55.2 us
    unnamed x2, local copies, waits for them, and re-layouts  1.27 us

profile of v3, /device:TPU:2, one launch (start us, length us, event | category | flops | bytes accessed | tf_op | source)
XLA Modules:
  0.0 57.1 jit_solution(391755763239448991)
XLA Ops:
  0.6 55.2 %modal_backward.1 = (bf16[128,512]{1,0:T(8,128)(2,1)S(1)}, f32[16,512]{1,0:T(8,128)S(1)}) custom-call(bf16[128,512]{1,0:T(8,128)(2,1)} %go.1, bf16[128,512]{1,0:T(8,128)(2,1)} %gate.1, bf16[128,512]{1,0:T(8,128)(2,1)} %conv.1, bf16[64,512]{1,0:T(8,128)(2,1)} %bitcast.1, f32[16,512]{1,0:T(8,128)} %residues.1, f32[16,512]{1,0:T(8,128)} %rates.1), custom_call_target="tpu_custom_call" | custom-call | tf_op jit(solution)/shard_map/modal_backward/pallas_call | solution.py:456
  55.8 0.7 %copy.10 = bf16[128,512]{1,0:T(8,128)(2,1)} copy(bf16[128,512]{1,0:T(8,128)(2,1)S(1)} %get-tuple-element.4) | data formatting | bytes 262144
  56.5 0.6 %copy.11 = f32[16,512]{1,0:T(8,128)} copy(f32[16,512]{1,0:T(8,128)S(1)} %get-tuple-element.5) | data formatting | bytes 65536

commit v4 on v3

--- a/solution.py
+++ b/solution.py
@@ -17,6 +17,7 @@
 LANES = 128
 SEG = 64
 LENGTH = 8192
+UNROLL = 4
 HOPS = {0: (2, 1), 2: (2, 1), 4: (2, 1), 6: (2, 1)}
 
 
@@ -24,9 +25,9 @@
     go, gate, conv, weight, residues, rates,
     out, rout,
     gobuf, wbuf, gtcv, rt, rs, rt_all, rs_all,
-    dec, resb, dec_all, resb_all, seg_all, gc, cvf, nearf, near, sent, arrived, sent_end, arrived_end,
+    dec, resb, dec_all, resb_all, seg_all, gc, cvf, nearf, near, heads, ends, sent, arrived, sent_end, arrived_end,
     inrow, inrow_in, backs, incoming, rowsum, rowsum_in, outf,
-    loc_sem, go_s, go_r, sib_r, z_s, z_r, gc_s, gc_r,
+    loc_sem, go_s, go_r, sib_r, z_s, z_r, leaf_r, y_r, gc_s, gc_r,
     a_s, a_r, e_s, e_r, i_s, i_r, n_s, n_r, b_s, b_r, t_s, t_r,
 ):
     ctx = lax.axis_index("ctx")
@@ -88,12 +89,16 @@
     pl.semaphore_wait(barrier, len(near_devices))
 
     def z_slot(way, r, far):
-        return r * NZ + (far if way else NZ - far)
+        return (r * 2 + way) * 3 + far // 2 - 1
 
     def z_send(way, r, owner, far, hop, src=None, to=None):
         ref = wbuf.at[piece(r, owner)]
         target = dev(dy=to, dz=up(-hop if way else hop))
-        send(ref if src is None else src, ref, z_s.at[0], z_r.at[z_slot(way, r, far)], target)
+        if far in HOPS:
+            sem = z_r.at[z_slot(way, r, far)]
+        else:
+            sem = leaf_r.at[0 if far < 6 else 1]
+        send(ref if src is None else src, ref, z_s.at[0], sem, target)
 
     def z_wait(way, r, far):
         wait(wbuf.at[piece(r, up(far if way else -far))], z_r.at[z_slot(way, r, far)])
@@ -106,7 +111,7 @@
                 z_send(way, r, z, hop, hop, src, to)
     for r in (1, 3, 2):
         to = (y + NY - r) % NY
-        send(weight.at[:, lanes(to)], wbuf.at[piece(r, z)], z_s.at[0], z_r.at[r * NZ], dev(dy=to))
+        send(weight.at[:, lanes(to)], wbuf.at[piece(r, z)], z_s.at[0], y_r.at[r], dev(dy=to))
 
     A, B = (0, 48), (48, 80)
     A0, A1, B0, B1 = (0, 32), (32, 16), (48, 48), (96, 32)
@@ -150,7 +155,7 @@
 
     def y_pieces():
         for r in (1, 3, 2):
-            wait(wbuf.at[piece(r, z)], z_r.at[r * NZ])
+            wait(wbuf.at[piece(r, z)], y_r.at[r])
             for way in (0, 1):
                 z_send(way, r, z, 1, 1)
 
@@ -241,14 +246,20 @@
 
     zeros = tuple(jnp.zeros((8, LANES), F32) for _ in range(MODES))
 
-    def end_step(t, sums):
+    def head_step(t, sums):
         c = cvf[pl.ds(t, 8, stride=SEG), :]
-        return tuple(dec[m] * (s + c) for m, s in enumerate(sums))
+        sums = tuple(dec[m] * s + c for m, s in enumerate(sums))
+        for m, s in enumerate(sums):
+            heads[t, m] = s
+        return sums
 
     def input_ends():
         wait(gtcv.at[pl.ds(0, 6)], gc_r.at[0])
         cvf[...] = gtcv[NY : 2 * NY].reshape(NY * ROWS, LANES).astype(F32)
-        sums = lax.fori_loop(0, SEG, end_step, zeros)
+        sums = lax.fori_loop(0, SEG, head_step, zeros)
+        sums = [dec[m] * s for m, s in enumerate(sums)]
+        for m, s in enumerate(sums):
+            ends[m] = s
         for p in range(half_modes):
             s, o = sums[p], sums[p + half_modes]
             sent_end[p] = jnp.where(even, next_up(s) + by_seg(p) * s, o + by_seg(p + half_modes) * next_down(o))
@@ -258,12 +269,8 @@
         for d in chips:
             send(sent_end.at[up(d) % half_modes], arrived_end.at[z], e_s.at[0], e_r.at[0], dev(dz=up(d)))
 
-    def z_leaves(fars):
-        for far in fars:
-            for r in range(NY):
-                for way in (0, 1):
-                    if far < 8 or way == r % 2:
-                        z_wait(way, r, far)
+    def z_leaves(group):
+        wait(wbuf.at[pl.ds(0, 24 if group == 0 else 12)], leaf_r.at[group])
 
     z_round(2, (0,))
     turn(0)
@@ -286,11 +293,11 @@
     z_round(6, (0, 1))
     far_shards(0)
     z_round(6, (3, 2))
-    z_leaves((1, 3, 5))
+    z_leaves(0)
     send_ends((6, -6, 5, -5, 4, -4, 3, -3, 2, -2, 1, -1))
     far_shards(1)
     far_shards(2)
-    z_leaves((7, 8))
+    z_leaves(1)
     send_ends((8, 7, -7))
     wait(gobuf.at[pl.ds(0, NX * NY)], sib_r.at[0])
 
@@ -307,7 +314,7 @@
         g = gc[pl.ds(SEG - 1 - i, 8, stride=SEG), :]
         return tuple(dec[m] * s + g for m, s in enumerate(sums))
 
-    sums = lax.fori_loop(0, SEG, start_step, zeros)
+    sums = lax.fori_loop(0, SEG, start_step, zeros, unroll=UNROLL)
     for p in range(half_modes):
         s, o = sums[p], sums[p + half_modes]
         sent[p] = jnp.where(even, s + by_seg(p) * next_up(s), next_down(o) + by_seg(p + half_modes) * o)
@@ -315,15 +322,13 @@
     arrived[z] = sent[z % half_modes]
     for d in far_first:
         send(sent.at[up(d) % half_modes], arrived.at[z], a_s.at[0], a_r.at[0], dev(dz=up(d)))
-    def inner_step(i, carry):
-        sums, inner = carry
-        g = gc[pl.ds(SEG - 1 - i, 8, stride=SEG), :]
-        c = cvf[pl.ds(SEG - 1 - i, 8, stride=SEG), :]
-        sums = tuple(dec[m] * s + g for m, s in enumerate(sums))
-        return sums, tuple(n + c * s for n, s in zip(inner, sums))
-
+    def inner_step(t, inner):
+        g = gc[pl.ds(t, 8, stride=SEG), :]
+        return tuple(n + g * heads[t, m] for m, n in enumerate(inner))
+
+    inner = lax.fori_loop(0, SEG, inner_step, zeros, unroll=UNROLL)
     from_second = tuple(jnp.where(even, next_up(s), 0.0) for s in sums)
-    _, inner = lax.fori_loop(0, SEG, inner_step, (from_second, zeros))
+    inner = [n + ends[m] * s for m, (n, s) in enumerate(zip(inner, from_second))]
     for m in range(MODES):
         inrow[m % half_modes, m // half_modes : m // half_modes + 1, :] = jnp.sum(inner[m], axis=0, keepdims=True)
     inrow_in[z] = inrow[z % half_modes]
@@ -340,7 +345,7 @@
         nearf[pl.ds(t, 8, stride=SEG), :] = acc
         return sums
 
-    lax.fori_loop(0, SEG, near_step, from_second)
+    lax.fori_loop(0, SEG, near_step, from_second, unroll=UNROLL)
     for r in (2, 1, 3):
         to = (y + r) % NY
         rows = pl.ds(pl.multiple_of(to * ROWS, ROWS), ROWS)
@@ -419,7 +424,7 @@
         outf[pl.ds(t, 8, stride=SEG), :] = acc
         return sums
 
-    lax.fori_loop(0, SEG, far_step, tuple(carried))
+    lax.fori_loop(0, SEG, far_step, tuple(carried), unroll=UNROLL)
     for q in range(NY):
         out[:, q * LANES : (q + 1) * LANES] = outf[q * ROWS : (q + 1) * ROWS, :].astype(BF16)
 
@@ -479,6 +484,8 @@
             f32(NY * ROWS, LANES),
             f32(NY * ROWS, LANES),
             f32(NY * ROWS, LANES),
+            f32(SEG, MODES, 8, LANES),
+            f32(MODES, 8, LANES),
             f32(MODES // 2, 8, LANES),
             f32(NZ, 8, LANES),
             f32(MODES // 2, 8, LANES),
@@ -492,7 +499,7 @@
             f32(NY * ROWS, LANES),
             dma((8,)),
             dma((1,)), dma((30,)), dma((1,)),
-            dma((1,)), dma((NY * NZ,)),
+            dma((1,)), dma((24,)), dma((2,)), dma((4,)),
             dma((1,)), dma((1,)),
             dma((1,)), dma((1,)),
             dma((1,)), dma((1,)),

time: 57.2 us -> 54.9 us (0.960)
  Pallas kernels: 55.2 us -> 52.9 us
    pallas_call x1, Pallas kernels: 55.2 us -> 52.9 us  [local(): pl.pallas_call(kernel, name='modal_backward', out_shape=(jax.ShapeDtypeSt...]
where the time goes in v4:
time: 54.9 us; the launch traced here: 54.8 us
  Pallas kernels  52.9 us (96%)
  local copies, waits for them, and re-layouts  1.27 us (2%)
  between operations  0.64 us (1%)
    pallas_call x1, Pallas kernels, local(): pl.pallas_call(kernel, name='modal_backward', out_shape=(jax.ShapeDtypeSt...  52.9 us
    unnamed x2, local copies, waits for them, and re-layouts  1.27 us

profile of v4, /device:TPU:2, one launch (start us, length us, event | category | flops | bytes accessed | tf_op | source)
XLA Modules:
  0.0 54.8 jit_solution(16979232814996562676)
XLA Ops:
  0.6 52.9 %modal_backward.1 = (bf16[128,512]{1,0:T(8,128)(2,1)S(1)}, f32[16,512]{1,0:T(8,128)S(1)}) custom-call(bf16[128,512]{1,0:T(8,128)(2,1)} %go.1, bf16[128,512]{1,0:T(8,128)(2,1)} %gate.1, bf16[128,512]{1,0:T(8,128)(2,1)} %conv.1, bf16[64,512]{1,0:T(8,128)(2,1)} %bitcast.1, f32[16,512]{1,0:T(8,128)} %residues.1, f32[16,512]{1,0:T(8,128)} %rates.1), custom_call_target="tpu_custom_call" | custom-call | tf_op jit(solution)/shard_map/modal_backward/pallas_call | solution.py:461
  53.5 0.7 %copy.10 = bf16[128,512]{1,0:T(8,128)(2,1)} copy(bf16[128,512]{1,0:T(8,128)(2,1)S(1)} %get-tuple-element.4) | data formatting | bytes 262144
  54.2 0.6 %copy.11 = f32[16,512]{1,0:T(8,128)} copy(f32[16,512]{1,0:T(8,128)S(1)} %get-tuple-element.5) | data formatting | bytes 65536

commit v5 on v4

--- a/solution.py
+++ b/solution.py
@@ -49,8 +49,7 @@
 
     near_devices = [dev(dx=xp), dev(dx=xm), dev(dx=x2), dev(dk=1 - k)]
     near_devices += [dev(dz=up(n)) for n in (1, -1, 2, -2)]
-    for yy in (yp, ym, y2):
-        near_devices += [dev(dy=yy, dz=up(n)) for n in (0, 2, -2)]
+    near_devices += [dev(dy=yy) for yy in (yp, ym, y2)]
     barrier = pltpu.get_barrier_semaphore()
     for d in near_devices:
         pl.semaphore_signal(barrier, inc=1, device_id=d, device_id_type=MESH)
@@ -106,7 +105,7 @@
     for r in (0, 1, 3, 2):
         to = (y + NY - r) % NY
         src = weight.at[:, lanes(to)]
-        for hop in HOPS[0] if r == 0 else HOPS[0][:1]:
+        for hop in HOPS[0] if r == 0 else ():
             for way in (0, 1):
                 z_send(way, r, z, hop, hop, src, to)
     for r in (1, 3, 2):
@@ -156,8 +155,9 @@
     def y_pieces():
         for r in (1, 3, 2):
             wait(wbuf.at[piece(r, z)], y_r.at[r])
-            for way in (0, 1):
-                z_send(way, r, z, 1, 1)
+            for hop in HOPS[0]:
+                for way in (0, 1):
+                    z_send(way, r, z, hop, hop)
 
     columns = (("L", xm), ("R", xp), ("X2", x2))
     lines_ = (("D", ym), ("U", yp), ("Y2", y2))
@@ -272,17 +272,17 @@
     def z_leaves(group):
         wait(wbuf.at[pl.ds(0, 24 if group == 0 else 12)], leaf_r.at[group])
 
+    y_pieces()
     z_round(2, (0,))
     turn(0)
     turn(1)
     z_round(2, (1, 3, 2))
-    y_pieces()
     turn(2)
-    gates()
     decays()
     near_shards(0)
     near_shards(1)
     near_shards(2)
+    gates()
     z_round(4, (0, 1))
     onward(0)
     z_round(4, (3, 2))

time: 54.9 us -> 52.8 us (0.962)
  the two profiles are of different devices: /device:TPU:2 before, /device:TPU:8 now
where the time goes in v5:
time: 52.8 us; the launch traced here: 52.7 us
  Pallas kernels  50.8 us (96%)
  local copies, waits for them, and re-layouts  1.27 us (2%)
  between operations  0.64 us (1%)
    pallas_call x1, Pallas kernels, local(): pl.pallas_call(kernel, name='modal_backward', out_shape=(jax.ShapeDtypeSt...  50.8 us
    unnamed x2, local copies, waits for them, and re-layouts  1.27 us

profile of v5, /device:TPU:8, one launch (start us, length us, event | category | flops | bytes accessed | tf_op | source)
XLA Modules:
  0.0 52.7 jit_solution(17100348303038474985)
XLA Ops:
  0.6 50.8 %modal_backward.1 = (bf16[128,512]{1,0:T(8,128)(2,1)S(1)}, f32[16,512]{1,0:T(8,128)S(1)}) custom-call(bf16[128,512]{1,0:T(8,128)(2,1)} %go.1, bf16[128,512]{1,0:T(8,128)(2,1)} %gate.1, bf16[128,512]{1,0:T(8,128)(2,1)} %conv.1, bf16[64,512]{1,0:T(8,128)(2,1)} %bitcast.1, f32[16,512]{1,0:T(8,128)} %residues.1, f32[16,512]{1,0:T(8,128)} %rates.1), custom_call_target="tpu_custom_call" | custom-call | tf_op jit(solution)/shard_map/modal_backward/pallas_call | solution.py:461
  51.4 0.7 %copy.10 = bf16[128,512]{1,0:T(8,128)(2,1)} copy(bf16[128,512]{1,0:T(8,128)(2,1)S(1)} %get-tuple-element.4) | data formatting | bytes 262144
  52.1 0.6 %copy.11 = f32[16,512]{1,0:T(8,128)} copy(f32[16,512]{1,0:T(8,128)S(1)} %get-tuple-element.5) | data formatting | bytes 65536

commit v6 on v5

--- a/solution.py
+++ b/solution.py
@@ -26,7 +26,7 @@
     out, rout,
     gobuf, wbuf, gtcv, rt, rs, rt_all, rs_all,
     dec, resb, dec_all, resb_all, seg_all, gc, cvf, nearf, near, heads, ends, sent, arrived, sent_end, arrived_end,
-    inrow, inrow_in, backs, incoming, rowsum, rowsum_in, outf,
+    inrow, inrow_in, backs, late_all, incoming, rowsum, rowsum_in, outf,
     loc_sem, go_s, go_r, sib_r, z_s, z_r, leaf_r, y_r, gc_s, gc_r,
     a_s, a_r, e_s, e_r, i_s, i_r, n_s, n_r, b_s, b_r, t_s, t_r,
 ):
@@ -289,8 +289,8 @@
     onward(1)
     diagonal_shards()
     onward(2)
+    z_round(6, (0, 1))
     input_ends()
-    z_round(6, (0, 1))
     far_shards(0)
     z_round(6, (3, 2))
     z_leaves(0)
@@ -375,17 +375,20 @@
     ins = []
     for zz in range(NZ):
         ins.append(after[zz] + to_line[zz] * lines)
-        for b in range(NY):
-            backs[zz * NY + b] = ins[zz][2 * b : 2 * b + 2]
+        late_all[zz] = ins[zz]
 
     served = (-4, 3, -3, 2, -2, 1, -1, 0)
     slot = pair * NY + y
-    incoming[slot] = backs[z * NY + y]
-    for d in served:
+    for i, d in enumerate(served):
+        late = late_all[up(d)]
+        for b in range(NY):
+            backs[i * NY + b] = late[2 * b : 2 * b + 2]
+        if d == 0:
+            incoming[slot] = backs[i * NY + y]
         for r in (2, 1, 3, 0):
             if d or r:
                 to = (y + r) % NY
-                send(backs.at[up(d) * NY + to], incoming.at[slot], b_s.at[0], b_r.at[0], dev(dy=to, dz=up(d)))
+                send(backs.at[i * NY + to], incoming.at[slot], b_s.at[0], b_r.at[0], dev(dy=to, dz=up(d)))
 
     wait(arrived_end.at[pl.ds(0, NZ - 1)], e_r.at[0])
     grad = jnp.zeros((8, LANES), F32)
@@ -492,7 +495,8 @@
             f32(NZ, 8, LANES),
             f32(MODES // 2, 2, LANES),
             f32(NZ, 2, LANES),
-            f32(NZ * NY, 2, LANES),
+            f32(MODES // 2 * NY, 2, LANES),
+            f32(NZ, 8, LANES),
             f32(MODES // 2 * NY, 2, LANES),
             f32(2, LANES),
             f32(MODES // 2 * NY, 2, LANES),

time: 52.8 us -> 52.8 us (level)
  the two profiles are of different devices: /device:TPU:8 before, /device:TPU:2 now
where the time goes in v6:
time: 52.8 us; the launch traced here: 52.7 us
  Pallas kernels  50.7 us (96%)
  local copies, waits for them, and re-layouts  1.27 us (2%)
  between operations  0.64 us (1%)
    pallas_call x1, Pallas kernels, local(): pl.pallas_call(kernel, name='modal_backward', out_shape=(jax.ShapeDtypeSt...  50.7 us
    unnamed x2, local copies, waits for them, and re-layouts  1.27 us

profile of v6, /device:TPU:2, one launch (start us, length us, event | category | flops | bytes accessed | tf_op | source)
XLA Modules:
  0.0 52.7 jit_solution(12145466069344619957)
XLA Ops:
  0.6 50.7 %modal_backward.1 = (bf16[128,512]{1,0:T(8,128)(2,1)S(1)}, f32[16,512]{1,0:T(8,128)S(1)}) custom-call(bf16[128,512]{1,0:T(8,128)(2,1)} %go.1, bf16[128,512]{1,0:T(8,128)(2,1)} %gate.1, bf16[128,512]{1,0:T(8,128)(2,1)} %conv.1, bf16[64,512]{1,0:T(8,128)(2,1)} %bitcast.1, f32[16,512]{1,0:T(8,128)} %residues.1, f32[16,512]{1,0:T(8,128)} %rates.1), custom_call_target="tpu_custom_call" | custom-call | tf_op jit(solution)/shard_map/modal_backward/pallas_call | solution.py:464
  51.4 0.7 %copy.10 = bf16[128,512]{1,0:T(8,128)(2,1)} copy(bf16[128,512]{1,0:T(8,128)(2,1)S(1)} %get-tuple-element.4) | data formatting | bytes 262144
  52.0 0.6 %copy.11 = f32[16,512]{1,0:T(8,128)} copy(f32[16,512]{1,0:T(8,128)S(1)} %get-tuple-element.5) | data formatting | bytes 65536

commit v7 on v6

--- a/solution.py
+++ b/solution.py
@@ -208,9 +208,16 @@
         go_wait((key, "Y2"), ox, y2, A)
         if i < 2:
             sibling(ox, y2)
+        else:
+            ref = go_ref(x2, y2, A)
+            send(ref, ref, go_s.at[0], sib_r.at[0], dev(dk=1 - k))
         key, oy = lines_[i]
         go_wait((key, "X2"), x2, oy, B)
-        sibling(x2, oy)
+        if i < 2:
+            sibling(x2, oy)
+        else:
+            ref = go_ref(x2, y2, B)
+            send(ref, ref, go_s.at[0], sib_r.at[0], dev(dk=1 - k))
 
     def spread(ref, m):
         rows = [jnp.broadcast_to(ref[m : m + 1, q * LANES : (q + 1) * LANES], (2, LANES)) for q in range(NY)]

time: 52.8 us -> 52.8 us (level)
  no operation moved by 1% of the time
where the time goes in v7:
time: 52.8 us; the launch traced here: 52.7 us
  Pallas kernels  50.8 us (96%)
  local copies, waits for them, and re-layouts  1.27 us (2%)
  between operations  0.64 us (1%)
    pallas_call x1, Pallas kernels, local(): pl.pallas_call(kernel, name='modal_backward', out_shape=(jax.ShapeDtypeSt...  50.8 us
    unnamed x2, local copies, waits for them, and re-layouts  1.27 us

profile of v7, /device:TPU:2, one launch (start us, length us, event | category | flops | bytes accessed | tf_op | source)
XLA Modules:
  0.0 52.7 jit_solution(17419058662917861034)
XLA Ops:
  0.6 50.8 %modal_backward.1 = (bf16[128,512]{1,0:T(8,128)(2,1)S(1)}, f32[16,512]{1,0:T(8,128)S(1)}) custom-call(bf16[128,512]{1,0:T(8,128)(2,1)} %go.1, bf16[128,512]{1,0:T(8,128)(2,1)} %gate.1, bf16[128,512]{1,0:T(8,128)(2,1)} %conv.1, bf16[64,512]{1,0:T(8,128)(2,1)} %bitcast.1, f32[16,512]{1,0:T(8,128)} %residues.1, f32[16,512]{1,0:T(8,128)} %rates.1), custom_call_target="tpu_custom_call" | custom-call | tf_op jit(solution)/shard_map/modal_backward/pallas_call | solution.py:471
  51.4 0.7 %copy.10 = bf16[128,512]{1,0:T(8,128)(2,1)} copy(bf16[128,512]{1,0:T(8,128)(2,1)S(1)} %get-tuple-element.4) | data formatting | bytes 262144
  52.0 0.6 %copy.11 = f32[16,512]{1,0:T(8,128)} copy(f32[16,512]{1,0:T(8,128)S(1)} %get-tuple-element.5) | data formatting | bytes 65536
